TPU v7x, 256 devices: a whole 4x4x8 slice. The times are simulated.
256 devices in a mesh: stream: 8 (over x, z_lo), tm: 32 (over z_hi, y, core).
Axes of the slice: x: 4, y: 4, z: 8 (z_hi: 4, z_lo: 2; z = z_hi * 2 + z_lo), core: 2. Of those that a mesh axis runs over, the one named last changes fastest.
Arguments:
- latents: bfloat16 [128, 64, 1024], P('stream'), may hold values from -6 to 6
- cache_prev: bfloat16 [128, 8, 1024], P('stream', None, 'tm'), may hold values from -6 to 6
- prev_slot: int32 [128], P('stream'), may hold values from 0 to 127, each once
- lengths: int32 [128], P('stream'), may hold values from 1 to 64, as said below
- conv_in_w: bfloat16 [7, 1024, 1536], P(None, None, 'tm'), may hold values from -0.0625 to 0.0625
- upsample_w: bfloat16 [16, 1536, 768], P(None, None, 'tm'), may hold values from -0.109375 to 0.109375
- alpha_coarse: float32 [1536], P('tm'), may hold values from 0.3 to 3
- alpha_in: float32 [768], replicated, may hold values from 0.3 to 3
- alpha_mid: float32 [768], replicated, may hold values from 0.3 to 3
- dilated_w: bfloat16 [7, 768, 768], P(None, 'tm'), may hold values from -0.078125 to 0.078125
- project_w: bfloat16 [768, 768], replicated, may hold values from -0.21875 to 0.21875
Outputs:
- decoded: bfloat16 [128, 512, 768], P('stream', 'tm')
Inputs may be any that keep to these rules, and one draw needn't show every extreme that they name: `prev_slot`: a permutation: every row of cache_prev belongs to exactly one stream. `lengths`: some stream runs through the whole window.
All inputs are finite; a program needn't handle non-finite values.
Results may differ from a plain program's by a relative error of at most 0.0085.
Values may be sent and summed in bfloat16 or wider, within the bound.
No kernel may reach another device: no remote copies, remote signals or barrier semaphores. Data moves between devices by JAX's collectives and lax.ppermute only.
A program may use at most 128 MiB of HBM per device.

v0:
```python
import functools

import jax
import jax.numpy as jnp
from jax import lax
from jax.experimental import pallas as pl
from jax.experimental.pallas import tpu as pltpu
from jax.sharding import PartitionSpec as P

F32 = jnp.float32
BF16 = jnp.bfloat16
VMEM_LIMIT = 48 * 1024 * 1024


def sin_squared(u):
    k = jnp.floor(u * 0.3183098861837907 + 0.5)
    r = u - k * 3.140625
    r = r - k * 0.0009670257568359375
    r = r - k * 6.2771141529083252e-07
    r = jnp.clip(r, -1.5708, 1.5708)
    q = r * r
    p = -2.5052108385441720e-08
    p = p * q + 2.7557319223985893e-06
    p = p * q - 1.9841269841269841e-04
    p = p * q + 8.3333333333333333e-03
    p = p * q - 1.6666666666666667e-01
    s = r + r * (q * p)
    return s * s


def snake(x, alpha, inverse):
    return x + sin_squared(alpha * x) * inverse


def fill_taps(w_ref, wc_ref):
    taps, _, width = w_ref.shape
    wc_ref[...] = jnp.zeros_like(wc_ref)
    for k in range(taps):
        at = 64 * k
        wc_ref[:, at : at + width] = w_ref[k]


def tap_sum(y, shift, width):
    rows = y.shape[0]
    total = None
    for g in range(y.shape[1] // 128):
        part = y[:, 128 * g : 128 * g + 128]
        turn = (-(2 * g + shift)) % rows
        if turn:
            part = pltpu.roll(part, turn, 0)
        total = part if total is None else total + part
    odd = pltpu.roll(pltpu.roll(total, rows - 1, 0), 64, 1)
    return total + odd


def coarse_kernel(order_ref, lat_ref, w_ref, a_ref, ia_ref, out_ref, wc_ref, v_ref):
    half, frames, depth = lat_ref.shape
    width = out_ref.shape[1]

    @pl.when(pl.program_id(0) == 0)
    def _():
        fill_taps(w_ref, wc_ref)

    x = lat_ref[...].reshape(half * frames, depth)
    y = jnp.dot(x, wc_ref[...], preferred_element_type=F32)
    for s in range(half):
        v_ref[s * frames : (s + 1) * frames, :] = tap_sum(
            y[s * frames : (s + 1) * frames], -6, width
        )
    u = [v_ref[pl.ds(t, half, stride=frames), :] for t in range(frames)]
    u = jnp.concatenate(u, axis=0)
    u = snake(u, a_ref[...], ia_ref[...])
    out_ref[0] = u.T[:width].astype(BF16)


def history_kernel(h_ref, lat_ref, w_ref, a_ref, ia_ref, out_ref, wc_ref, v_ref):
    streams, frames, depth = lat_ref.shape
    width = out_ref.shape[1]
    past = h_ref.shape[1] // streams
    half = streams // 2
    fill_taps(w_ref, wc_ref)
    wc = wc_ref[...]
    ht = h_ref[...].astype(F32).T.astype(BF16)
    yh = jnp.dot(ht, wc, preferred_element_type=F32)
    yl = jnp.dot(
        lat_ref[...].reshape(streams * frames, depth), wc, preferred_element_type=F32
    )
    for s in range(streams):
        z = jnp.concatenate(
            [yh[past * s : past * (s + 1)], yl[frames * s : frames * s + past]], axis=0
        )
        v_ref[past * s : past * (s + 1), :] = tap_sum(z, 0, width)[:past]
    for c in range(2):
        rows = [
            v_ref[pl.ds(c * half * past + i, half, stride=past), :] for i in range(past)
        ]
        gap = jnp.zeros((128 - past * half, 128), F32)
        u = jnp.concatenate(rows[2:] + [gap] + rows[:2], axis=0)
        u = snake(u, a_ref[...], ia_ref[...])
        out_ref[c] = u.T[:width].astype(BF16)


def upsample_kernel(off_ref, x0, x1, x2, x3, xh_ref, w_ref, out_ref, xs_ref, fs_ref):
    width = 48
    n = x0.shape[1]
    pieces = x0.shape[0] // width
    for dy, ref in enumerate((x0, x1, x2, x3)):
        for i in range(pieces):
            at = pl.multiple_of(off_ref[dy * pieces + i], 16)
            xs_ref[pl.ds(at, width), :] = ref[i * width : (i + 1) * width, :]
    rows = w_ref.shape[0]
    half = rows // 2
    r = jnp.dot(w_ref[...], xs_ref[...], preferred_element_type=F32)
    rh = jnp.dot(w_ref[...], xh_ref[...], preferred_element_type=F32)
    lane = lax.broadcasted_iota(jnp.int32, (rows, 128), 1)
    first = jnp.where(lane < 48, rh, r[:, :128])
    r = jnp.concatenate([first, r[:, 128:]], axis=1)
    turned = pltpu.roll(rh[half:], 8, 1)
    shifted = pltpu.roll(r[half:], 8, 1)
    lane = lax.broadcasted_iota(jnp.int32, (half, 128), 1)
    shifted = jnp.concatenate(
        [jnp.where(lane < 8, turned, shifted[:, :128]), shifted[:, 128:]], axis=1
    )
    fs_ref[8 : 8 + n, :] = (r[:half] + shifted).T
    fs_ref[0:8, :] = (rh[:half] + turned).T[120:128]
    blocks, take, _ = out_ref.shape
    for b in range(blocks):
        out_ref[b] = fs_ref[16 * b : 16 * b + take, :].astype(BF16)


def residual_kernel(
    arr_ref, lim_ref, ai_ref, iai_ref, am_ref, iam_ref, wd_ref, wp_ref,
    out_ref, f_ref, win_ref, acc_ref, r_ref,
):
    k = pl.program_id(0)
    taps = pl.num_programs(0)
    rows, channels = acc_ref.shape
    streams = out_ref.shape[0]
    sources, take, _ = arr_ref.shape
    piece = 48
    half = streams // 2

    @pl.when(k == 0)
    def _():
        for c in range(2):
            for j in range(8):
                x = jnp.concatenate(
                    [
                        arr_ref[m, :, piece * j : piece * (j + 1)].astype(F32)
                        for m in range(c, sources, 2)
                    ],
                    axis=1,
                )
                for t in range(take // half):
                    at = (8 * t + j) * streams + half * c
                    f_ref[at : at + half, :] = x[half * t : half * (t + 1)]
        win_ref[...] = snake(f_ref[...], ai_ref[...], iai_ref[...]).astype(BF16)
        acc_ref[...] = jnp.zeros_like(acc_ref)

    at = pl.multiple_of((k + 2) * streams, 16)
    acc_ref[...] += jnp.dot(
        win_ref[pl.ds(at, rows), :], wd_ref[0], preferred_element_type=F32
    )

    @pl.when(k == taps - 1)
    def _():
        middle = snake(acc_ref[...], am_ref[...], iam_ref[...]).astype(BF16)
        summed = f_ref[8 * streams :, :] + jnp.dot(
            middle, wp_ref[...], preferred_element_type=F32
        )
        local = lax.broadcasted_iota(jnp.int32, (rows, channels), 0) // streams
        kept = jnp.where(local < lim_ref[...], summed, 0.0)
        for g in range(channels // 128):
            r_ref[g] = kept[:, 128 * g : 128 * (g + 1)]
        for s in range(streams):
            out_ref[s] = jnp.concatenate(
                [
                    r_ref[g, pl.ds(s, rows // streams, stride=streams), :]
                    for g in range(channels // 128)
                ],
                axis=1,
            ).astype(BF16)


def whole(*shape):
    return pl.BlockSpec(shape, lambda *_: (0,) * len(shape))


def per_device(
    latents,
    cache_prev,
    prev_slot,
    lengths,
    conv_in_w,
    upsample_w,
    alpha_coarse,
    alpha_in,
    alpha_mid,
    dilated_w,
    project_w,
):
    groups, frames, depth = latents.shape
    taps, _, width = conv_in_w.shape
    past = cache_prev.shape[1]
    slab = cache_prev.shape[2]
    half = groups // 2
    channels = dilated_w.shape[2]
    tm = lax.axis_index("tm")
    z, y, core = tm // 8, (tm // 2) % 4, tm % 2

    def turned(dz, dy, flip=0):
        pairs = []
        for m in range(32):
            a, b, c = m // 8, (m // 2) % 4, m % 2
            pairs.append((m, ((a + dz) % 4) * 8 + ((b + dy) % 4) * 2 + (c + flip) % 2))
        return pairs

    def send(x, dz, dy, flip=0):
        return lax.ppermute(x, "tm", turned(dz, dy, flip))

    dilated = lax.all_gather(dilated_w, "tm", axis=1, tiled=True)
    up_t = jnp.transpose(upsample_w, (0, 2, 1))
    up_other = send(up_t, 0, 0, 1)
    up = jnp.where(
        core == 0,
        jnp.concatenate([up_t, up_other], axis=1),
        jnp.concatenate([up_other, up_t], axis=1),
    ).reshape(-1, up_t.shape[2])

    flat = cache_prev.reshape(groups, past * slab)
    every = lax.all_to_all(
        jnp.broadcast_to(flat[None], (8,) + flat.shape), "stream", 0, 0, tiled=True
    ).reshape(8 * groups, past * slab)
    selected = jnp.take(every, prev_slot, axis=0).reshape(groups * past, slab).T
    history = lax.all_to_all(
        jnp.broadcast_to(selected[None], (32,) + selected.shape), "tm", 0, 0, tiled=True
    ).reshape(32 * slab, groups * past)

    pad = 128 - width
    alpha_c = jnp.pad(alpha_coarse, (0, pad), constant_values=1.0)[None]
    inverse_c = 1.0 / alpha_c
    order = jnp.stack([core, 1 - core]).astype(jnp.int32)
    main = pl.pallas_call(
        coarse_kernel,
        grid_spec=pltpu.PrefetchScalarGridSpec(
            num_scalar_prefetch=1,
            grid=(2,),
            in_specs=[
                pl.BlockSpec((half, frames, depth), lambda i, o: (o[i], 0, 0)),
                whole(taps, depth, width),
                whole(1, 128),
                whole(1, 128),
            ],
            out_specs=pl.BlockSpec((1, width, half * frames), lambda i, o: (i, 0, 0)),
            scratch_shapes=[
                pltpu.VMEM((depth, 512), BF16),
                pltpu.VMEM((half * frames, 128), F32),
            ],
        ),
        out_shape=jax.ShapeDtypeStruct((2, width, half * frames), BF16),
        compiler_params=pltpu.CompilerParams(vmem_limit_bytes=VMEM_LIMIT),
        name="coarse_main",
    )(order, latents, conv_in_w, alpha_c, inverse_c)
    own = jnp.concatenate([main[0], send(main[1], 0, 0, 1)], axis=0)
    column = jnp.concatenate([own, send(own, 1, 0), send(own, 2, 0), send(own, 3, 0)], axis=0)
    columns = [column, send(column, 0, 1), send(column, 0, 2), send(column, 0, 3)]

    head = pl.pallas_call(
        history_kernel,
        grid=(1,),
        in_specs=[
            whole(depth, groups * past),
            whole(groups, 16, depth),
            whole(taps, depth, width),
            whole(1, 128),
            whole(1, 128),
        ],
        out_specs=whole(2, width, 128),
        out_shape=jax.ShapeDtypeStruct((2, width, 128), BF16),
        scratch_shapes=[pltpu.VMEM((depth, 512), BF16), pltpu.VMEM((groups * past, 128), F32)],
        compiler_params=pltpu.CompilerParams(vmem_limit_bytes=VMEM_LIMIT),
        name="coarse_history",
    )(history, latents, conv_in_w, alpha_c, inverse_c)
    heads = lax.all_to_all(
        jnp.tile(head, (16, 1, 1)), "tm", 0, 0, tiled=True
    ).reshape(32 * width, 128)

    offsets = []
    for dy in range(4):
        for dz in range(4):
            for flip in range(2):
                source = ((z - dz) % 4) * 8 + ((y - dy) % 4) * 2 + (core + flip) % 2
                offsets.append(source * width)
    offsets = jnp.stack(offsets).astype(jnp.int32)
    n = half * frames
    blocks = pl.pallas_call(
        upsample_kernel,
        grid_spec=pltpu.PrefetchScalarGridSpec(
            num_scalar_prefetch=1,
            grid=(1,),
            in_specs=[whole(8 * width, n)] * 4
            + [whole(32 * width, 128), whole(16 * width, 32 * width)],
            out_specs=whole(32, 24, 8 * width),
            scratch_shapes=[
                pltpu.VMEM((32 * width, n), BF16),
                pltpu.VMEM((n + 8, 8 * width), F32),
            ],
        ),
        out_shape=jax.ShapeDtypeStruct((32, 24, 8 * width), BF16),
        compiler_params=pltpu.CompilerParams(vmem_limit_bytes=VMEM_LIMIT),
        name="upsample",
    )(offsets, *columns, heads, up)
    arrived = lax.all_to_all(blocks, "tm", 0, 0, tiled=True)

    shard = 16
    rows = shard * groups
    limit = 8 * lengths - tm * shard
    limit = jnp.tile(limit, shard)[:, None].astype(jnp.int32)
    return pl.pallas_call(
        residual_kernel,
        grid=(taps,),
        in_specs=[
            whole(32, 24, 8 * width),
            whole(rows, 1),
            whole(1, channels),
            whole(1, channels),
            whole(1, channels),
            whole(1, channels),
            pl.BlockSpec((1, channels, channels), lambda k: (k, 0, 0)),
            whole(channels, channels),
        ],
        out_specs=whole(groups, shard, channels),
        out_shape=jax.ShapeDtypeStruct((groups, shard, channels), BF16),
        scratch_shapes=[
            pltpu.VMEM((24 * groups, channels), F32),
            pltpu.VMEM((24 * groups, channels), BF16),
            pltpu.VMEM((rows, channels), F32),
            pltpu.VMEM((channels // 128, rows, 128), F32),
        ],
        compiler_params=pltpu.CompilerParams(vmem_limit_bytes=VMEM_LIMIT),
        name="residual",
    )(
        arrived,
        limit,
        alpha_in[None],
        (1.0 / alpha_in)[None],
        alpha_mid[None],
        (1.0 / alpha_mid)[None],
        dilated,
        project_w,
    )


def solution(mesh):
    return jax.shard_map(
        per_device,
        mesh=mesh,
        in_specs=(
            P("stream", None, None),
            P("stream", None, "tm"),
            P("stream"),
            P("stream"),
            P(None, None, "tm"),
            P(None, None, "tm"),
            P("tm"),
            P(),
            P(),
            P(None, "tm", None),
            P(),
        ),
        out_specs=P("stream", "tm", None),
        check_vma=False,
    )
```

profile of v0, /device:TPU:1, one launch (start us, length us, event | category | flops | bytes accessed | tf_op | source)
XLA Modules:
  0.0 146.6 jit_solution(5497236739996970532)
XLA Ops:
  6.5 0.0 all-gather.2.cloned.1.call-start
  6.5 0.7 all-gather.2.cloned.1.call-update
  7.3 3.3 %collective-permute-start.7 = (bf16[16,24,1536]{2,1,0:T(8,128)(2,1)}, bf16[16,24,1536]{2,1,0:T(8,128)(2,1)}, u32[]{:S(2)}, u32[]{:S(2)}) collective-permute-start(bf16[16,24,1536]{2,1,0:T(8,128)(2,1)} %bitcast.55), channel_id=1, source_target_pairs={{0,1},{1,0},{2,3},{3,2},{4,5},{5,4},{6,7},{7,6},{8,9},{9,8},{10,11... | collective-permute-start | bytes 3538952 | tf_op jit(solution)/shard_map/ppermute | solution.py:219
  10.6 0.9 broadcast_in_dim.48
  11.4 0.6 broadcast_in_dim.49
  12.1 3.6 %all-to-all-start = ((bf16[8,16,256]{2,1,0:T(8,128)(2,1)}), bf16[8,16,256]{2,1,0:T(8,128)(2,1)S(1)}, u32[]{:S(2)}, u32[]{:S(2)}) async-start(bf16[8,16,256]{2,1,0:T(8,128)(2,1)} %broadcast_in_dim.49), calls=%async_computation | async-start | bytes 131072 | tf_op jit(solution)/shard_map/all_to_all | solution.py:231
  15.7 0.7 divide_bitcast_fusion
  16.4 0.7 compare_select_fusion
  17.0 0.7 compare_and_fusion
  17.7 0.1 pad_add_fusion.order_ref
  17.8 1.9 %copy.15.w_ref = bf16[7,1024,48]{2,1,0:T(8,128)(2,1)S(1)} copy(bf16[7,1024,48]{1,2,0:T(8,128)(2,1)} %param.15) | data formatting | bytes 1376256 | tf_op args[4]
  19.6 0.1 broadcast_in_dim.45
  19.7 0.1 broadcast_in_dim.46
  19.8 0.0 copy-start
  19.8 1.6 %copy-done = bf16[16,64,1024]{2,1,0:T(8,128)(2,1)S(1)} copy-done((bf16[16,64,1024]{2,1,0:T(8,128)(2,1)S(1)}, bf16[16,64,1024]{2,1,0:T(8,128)(2,1)}, u32[]{:S(2)}) %copy-start) | copy-done | bytes 2097176
  21.4 3.3 %coarse_main.1 = bf16[2,48,512]{2,1,0:T(8,128)(2,1)S(1)} custom-call(s32[2]{0:T(128)S(1)} %pad_add_fusion.order_ref, bf16[16,64,1024]{2,1,0:T(8,128)(2,1)S(1)} %copy-done, bf16[7,1024,48]{2,1,0:T(8,128)(2,1)S(1)} %copy.15.w_ref, f32[1,128]{1,0:T(1,128)S(1)} %get-tuple-element.8.a_ref, f32[1,128]{1,0:T(1,128)S(1)} %get-tuple-element.7.ia_ref), custom_call_target="tpu_custom_call" | custom-call | tf_op jit(solution)/shard_map/coarse_main/pallas_call | solution.py:243
  24.8 0.0 all-to-all-done
  24.8 0.6 gather_fusion
  25.4 0.1 gather.7
  25.5 0.1 select_bitcast_fusion
  25.5 0.1 copy.16
  25.6 0.8 broadcast_in_dim.52
  26.4 10.6 %all-to-all-start.1 = ((bf16[32,32,128]{2,1,0:T(8,128)(2,1)}), bf16[32,32,128]{2,1,0:T(8,128)(2,1)S(1)}, u32[]{:S(2)}, u32[]{:S(2)}) async-start(bf16[32,32,128]{2,1,0:T(8,128)(2,1)} %broadcast_in_dim.52), calls=%async_computation.1 | async-start | bytes 524288 | tf_op jit(solution)/shard_map/all_to_all | solution.py:235
  37.1 0.3 collective-permute-start
  37.4 1.0 collective-permute-done
  38.4 2.4 %collective-permute-start.1 = (bf16[96,512]{1,0:T(8,128)(2,1)S(1)}, bf16[96,512]{1,0:T(8,128)(2,1)S(1)}, u32[]{:S(2)}, u32[]{:S(2)}) collective-permute-start(bf16[96,512]{1,0:T(8,128)(2,1)S(1)} %pad_maximum_fusion), channel_id=1, source_target_pairs={{0,8},{1,9},{2,10},{3,11},{4,12},{5,13},{6,14},{7,15},{8,16},{9,17... | collective-permute-start | bytes 294920 | tf_op jit(solution)/shard_map/ppermute | solution.py:219
  40.7 3.3 %collective-permute-start.2 = (bf16[96,512]{1,0:T(8,128)(2,1)S(1)}, bf16[96,512]{1,0:T(8,128)(2,1)S(1)}, u32[]{:S(2)}, u32[]{:S(2)}) collective-permute-start(bf16[96,512]{1,0:T(8,128)(2,1)S(1)} %pad_maximum_fusion), channel_id=1, source_target_pairs={{0,16},{1,17},{2,18},{3,19},{4,20},{5,21},{6,22},{7,23},{8,24},{9,... | collective-permute-start | bytes 294920 | tf_op jit(solution)/shard_map/ppermute | solution.py:219
  44.1 3.3 %collective-permute-start.3 = (bf16[96,512]{1,0:T(8,128)(2,1)S(1)}, bf16[96,512]{1,0:T(8,128)(2,1)S(1)}, u32[]{:S(2)}, u32[]{:S(2)}) collective-permute-start(bf16[96,512]{1,0:T(8,128)(2,1)S(1)} %pad_maximum_fusion), channel_id=1, source_target_pairs={{0,24},{1,25},{2,26},{3,27},{4,28},{5,29},{6,30},{7,31},{8,0},{9,1... | collective-permute-start | bytes 294920 | tf_op jit(solution)/shard_map/ppermute | solution.py:219
  47.3 4.8 %all-to-all-done.1 = bf16[32,32,128]{2,1,0:T(8,128)(2,1)S(1)} async-done(((bf16[32,32,128]{2,1,0:T(8,128)(2,1)}), bf16[32,32,128]{2,1,0:T(8,128)(2,1)S(1)}, u32[]{:S(2)}, u32[]{:S(2)}) %all-to-all-start.1) | async-done | bytes 262176 | tf_op jit(solution)/shard_map/all_to_all | solution.py:235
  52.1 0.0 copy-start.1
  52.1 1.6 %copy-done.1 = bf16[16,64,1024]{2,1,0:T(8,128)(2,1)S(1)} copy-done((bf16[16,64,1024]{2,1,0:T(8,128)(2,1)S(1)}, bf16[16,64,1024]{2,1,0:T(8,128)(2,1)}, u32[]{:S(2)}) %copy-start.1) | copy-done | bytes 2097176
  53.7 1.3 coarse_history.1
  55.1 0.8 tile.6
  55.9 4.5 %all-to-all-start.2 = ((bf16[32,48,128]{2,1,0:T(8,128)(2,1)}), bf16[32,48,128]{2,1,0:T(8,128)(2,1)S(1)}, u32[]{:S(2)}, u32[]{:S(2)}) async-start(bf16[32,48,128]{2,1,0:T(8,128)(2,1)} %bitcast.41), calls=%async_computation.2 | async-start | bytes 786432 | tf_op jit(solution)/shard_map/all_to_all | solution.py:284
  60.4 0.0 collective-permute-done.1
  60.5 0.0 collective-permute-done.2
  60.5 0.0 collective-permute-done.3
  60.5 1.5 collective-permute-start.4
  62.0 2.4 %collective-permute-start.5 = (bf16[384,512]{1,0:T(8,128)(2,1)S(1)}, bf16[384,512]{1,0:T(8,128)(2,1)}, u32[]{:S(2)}, u32[]{:S(2)}) collective-permute-start(bf16[384,512]{1,0:T(8,128)(2,1)S(1)} %constant_dynamic-update-slice_fusion.x0), channel_id=1, source_target_pairs={{0,4},{1,5},{2,6},{3,7},{4,0},{5,1},{6,2},{7,3},{8,12},{9,13},{10,... | collective-permute-start | bytes 1179656 | tf_op jit(solution)/shard_map/ppermute | solution.py:219
  64.4 1.2 collective-permute-start.6
  65.6 0.1 stack.140.off_ref
  65.7 0.0 collective-permute-done.7
  65.7 3.1 %maximum_select_fusion = bf16[16,48,1536]{2,1,0:T(8,128)(2,1)S(1)} fusion(bf16[16,24,1536]{2,1,0:T(8,128)(2,1)} %collective-permute-done.7, bf16[16,24,1536]{2,1,0:T(8,128)(2,1)} %bitcast.56, pred[]{:T(512)S(6)} %eq.102), kind=kLoop, calls=%fused_computation.1 | loop fusion | flops 10616832 | bytes 4718593 | tf_op jit(solution)/shard_map/jit(_where)/select_n | solution.py:224
  68.7 11.3 %collective-permute-done.4.x1 = bf16[384,512]{1,0:T(8,128)(2,1)S(1)} collective-permute-done((bf16[384,512]{1,0:T(8,128)(2,1)S(1)}, bf16[384,512]{1,0:T(8,128)(2,1)S(1)}, u32[]{:S(2)}, u32[]{:S(2)}) %collective-permute-start.4) | collective-permute-done | bytes 393248 | tf_op jit(solution)/shard_map/ppermute | solution.py:219
  80.1 15.4 %collective-permute-done.5.x2 = bf16[384,512]{1,0:T(8,128)(2,1)} collective-permute-done((bf16[384,512]{1,0:T(8,128)(2,1)S(1)}, bf16[384,512]{1,0:T(8,128)(2,1)}, u32[]{:S(2)}, u32[]{:S(2)}) %collective-permute-start.5) | collective-permute-done | bytes 393248 | tf_op jit(solution)/shard_map/ppermute | solution.py:219
  95.4 0.4 collective-permute-done.6.x3
  95.9 0.0 all-to-all-done.2
  95.9 0.0 copy-start.5
  95.9 0.0 copy-start.3
  95.9 0.0 copy-start.4
  95.9 5.0 %upsample.1 = bf16[32,24,384]{2,1,0:T(8,128)(2,1)} custom-call(s32[32]{0:T(128)S(1)} %stack.140.off_ref, bf16[384,512]{1,0:T(8,128)(2,1)S(1)} %constant_dynamic-update-slice_fusion.x0, bf16[384,512]{1,0:T(8,128)(2,1)S(1)} %collective-permute-done.4.x1, bf16[384,512]{1,0:T(8,128)(2,1)} %collective-permute-done.5.x2, ...), custom_call_target="tpu_custom_call" | custom-call | tf_op jit(solution)/shard_map/upsample/pallas_call | solution.py:296
  100.9 8.9 %all-to-all-start.3 = ((bf16[32,24,384]{2,1,0:T(8,128)(2,1)}), bf16[32,24,384]{2,1,0:T(8,128)(2,1)S(1)}, u32[]{:S(2)}, u32[]{:S(2)}) async-start(bf16[32,24,384]{2,1,0:T(8,128)(2,1)} %upsample.1), calls=%async_computation.3 | async-start | bytes 1179648 | tf_op jit(solution)/shard_map/all_to_all | solution.py:313
  109.8 0.0 copy-done.5
  109.8 0.1 broadcast_in_dim_tile.4.lim_ref
  109.9 0.0 copy-done.3
  110.0 0.0 copy-done.4
  110.0 17.9 %all-to-all-done.3.arr_ref = bf16[32,24,384]{2,1,0:T(8,128)(2,1)S(1)} async-done(((bf16[32,24,384]{2,1,0:T(8,128)(2,1)}), bf16[32,24,384]{2,1,0:T(8,128)(2,1)S(1)}, u32[]{:S(2)}, u32[]{:S(2)}) %all-to-all-start.3) | async-done | bytes 589856 | tf_op jit(solution)/shard_map/all_to_all | solution.py:313
  127.9 0.0 all-gather.2.cloned.1.call-done.wd_ref
  128.0 0.0 copy-start.2
  128.0 1.3 copy-done.2
  129.2 10.6 %residual.1 = bf16[16,16,768]{2,1,0:T(8,128)(2,1)} custom-call(bf16[32,24,384]{2,1,0:T(8,128)(2,1)S(1)} %all-to-all-done.3.arr_ref, s32[256,1]{1,0:T(8,128)S(1)} %broadcast_in_dim_tile.4.lim_ref, f32[1,768]{1,0:T(1,128)S(1)} %broadcast_in_dim.53.ai_ref, f32[1,768]{1,0:T(1,128)S(1)} %broadcast_in_dim.54.iai_ref, f32[1,768]{1,0:T(1,128)S(1)} %broadcast_in_dim.55.am_ref, ...), custom_call_target="tpu_custom_call" | custom-call | tf_op jit(solution)/shard_map/residual/pallas_call | solution.py:319
  (16 shorter events, 0.1 us)
Async XLA Ops:
  6.5 121.4 %all-gather.2.cloned.1.call-start = ((), (), s32[]{:S(2)}) async-start(), calls=%async_computation.4 | async-start | bytes 8515584 | tf_op jit(solution)/shard_map/all_gather | solution.py:221
  7.3 58.4 %collective-permute-start.7 = (bf16[16,24,1536]{2,1,0:T(8,128)(2,1)}, bf16[16,24,1536]{2,1,0:T(8,128)(2,1)}, u32[]{:S(2)}, u32[]{:S(2)}) collective-permute-start(bf16[16,24,1536]{2,1,0:T(8,128)(2,1)} %bitcast.55), channel_id=1, source_target_pairs={{0,1},{1,0},{2,3},{3,2},{4,5},{5,4},{6,7},{7,6},{8,9},{9,8},{10,11... | collective-permute-start | bytes 3538952 | tf_op jit(solution)/shard_map/ppermute | solution.py:219
  12.1 12.7 %all-to-all-start = ((bf16[8,16,256]{2,1,0:T(8,128)(2,1)}), bf16[8,16,256]{2,1,0:T(8,128)(2,1)S(1)}, u32[]{:S(2)}, u32[]{:S(2)}) async-start(bf16[8,16,256]{2,1,0:T(8,128)(2,1)} %broadcast_in_dim.49), calls=%async_computation | async-start | bytes 131072 | tf_op jit(solution)/shard_map/all_to_all | solution.py:231
  19.8 1.6 %copy-start = (bf16[16,64,1024]{2,1,0:T(8,128)(2,1)S(1)}, bf16[16,64,1024]{2,1,0:T(8,128)(2,1)}, u32[]{:S(2)}) copy-start(bf16[16,64,1024]{2,1,0:T(8,128)(2,1)} %lat_ref.3) | copy-start | bytes 6291460
  26.4 25.8 %all-to-all-start.1 = ((bf16[32,32,128]{2,1,0:T(8,128)(2,1)}), bf16[32,32,128]{2,1,0:T(8,128)(2,1)S(1)}, u32[]{:S(2)}, u32[]{:S(2)}) async-start(bf16[32,32,128]{2,1,0:T(8,128)(2,1)} %broadcast_in_dim.52), calls=%async_computation.1 | async-start | bytes 524288 | tf_op jit(solution)/shard_map/all_to_all | solution.py:235
  37.1 1.3 collective-permute-start
  38.4 22.1 %collective-permute-start.1 = (bf16[96,512]{1,0:T(8,128)(2,1)S(1)}, bf16[96,512]{1,0:T(8,128)(2,1)S(1)}, u32[]{:S(2)}, u32[]{:S(2)}) collective-permute-start(bf16[96,512]{1,0:T(8,128)(2,1)S(1)} %pad_maximum_fusion), channel_id=1, source_target_pairs={{0,8},{1,9},{2,10},{3,11},{4,12},{5,13},{6,14},{7,15},{8,16},{9,17... | collective-permute-start | bytes 294920 | tf_op jit(solution)/shard_map/ppermute | solution.py:219
  40.7 19.7 %collective-permute-start.2 = (bf16[96,512]{1,0:T(8,128)(2,1)S(1)}, bf16[96,512]{1,0:T(8,128)(2,1)S(1)}, u32[]{:S(2)}, u32[]{:S(2)}) collective-permute-start(bf16[96,512]{1,0:T(8,128)(2,1)S(1)} %pad_maximum_fusion), channel_id=1, source_target_pairs={{0,16},{1,17},{2,18},{3,19},{4,20},{5,21},{6,22},{7,23},{8,24},{9,... | collective-permute-start | bytes 294920 | tf_op jit(solution)/shard_map/ppermute | solution.py:219
  44.1 16.4 %collective-permute-start.3 = (bf16[96,512]{1,0:T(8,128)(2,1)S(1)}, bf16[96,512]{1,0:T(8,128)(2,1)S(1)}, u32[]{:S(2)}, u32[]{:S(2)}) collective-permute-start(bf16[96,512]{1,0:T(8,128)(2,1)S(1)} %pad_maximum_fusion), channel_id=1, source_target_pairs={{0,24},{1,25},{2,26},{3,27},{4,28},{5,29},{6,30},{7,31},{8,0},{9,1... | collective-permute-start | bytes 294920 | tf_op jit(solution)/shard_map/ppermute | solution.py:219
  52.1 1.6 %copy-start.1 = (bf16[16,64,1024]{2,1,0:T(8,128)(2,1)S(1)}, bf16[16,64,1024]{2,1,0:T(8,128)(2,1)}, u32[]{:S(2)}) copy-start(bf16[16,64,1024]{2,1,0:T(8,128)(2,1)} %lat_ref.3) | copy-start | bytes 6291460
  55.9 40.0 %all-to-all-start.2 = ((bf16[32,48,128]{2,1,0:T(8,128)(2,1)}), bf16[32,48,128]{2,1,0:T(8,128)(2,1)S(1)}, u32[]{:S(2)}, u32[]{:S(2)}) async-start(bf16[32,48,128]{2,1,0:T(8,128)(2,1)} %bitcast.41), calls=%async_computation.2 | async-start | bytes 786432 | tf_op jit(solution)/shard_map/all_to_all | solution.py:284
  60.5 19.6 %collective-permute-start.4 = (bf16[384,512]{1,0:T(8,128)(2,1)S(1)}, bf16[384,512]{1,0:T(8,128)(2,1)S(1)}, u32[]{:S(2)}, u32[]{:S(2)}) collective-permute-start(bf16[384,512]{1,0:T(8,128)(2,1)S(1)} %constant_dynamic-update-slice_fusion.x0), channel_id=1, source_target_pairs={{0,2},{1,3},{2,4},{3,5},{4,6},{5,7},{6,0},{7,1},{8,10},{9,11},{10,... | collective-permute-start | bytes 1179656 | tf_op jit(solution)/shard_map/ppermute | solution.py:219
  62.0 33.5 %collective-permute-start.5 = (bf16[384,512]{1,0:T(8,128)(2,1)S(1)}, bf16[384,512]{1,0:T(8,128)(2,1)}, u32[]{:S(2)}, u32[]{:S(2)}) collective-permute-start(bf16[384,512]{1,0:T(8,128)(2,1)S(1)} %constant_dynamic-update-slice_fusion.x0), channel_id=1, source_target_pairs={{0,4},{1,5},{2,6},{3,7},{4,0},{5,1},{6,2},{7,3},{8,12},{9,13},{10,... | collective-permute-start | bytes 1179656 | tf_op jit(solution)/shard_map/ppermute | solution.py:219
  64.4 31.5 %collective-permute-start.6 = (bf16[384,512]{1,0:T(8,128)(2,1)S(1)}, bf16[384,512]{1,0:T(8,128)(2,1)}, u32[]{:S(2)}, u32[]{:S(2)}) collective-permute-start(bf16[384,512]{1,0:T(8,128)(2,1)S(1)} %constant_dynamic-update-slice_fusion.x0), channel_id=1, source_target_pairs={{0,6},{1,7},{2,0},{3,1},{4,2},{5,3},{6,4},{7,5},{8,14},{9,15},{10,... | collective-permute-start | bytes 1179656 | tf_op jit(solution)/shard_map/ppermute | solution.py:219
  95.9 13.9 %copy-start.5 = (s32[16]{0:T(128)S(1)}, s32[16]{0:T(128)}, u32[]{:S(2)}) copy-start(s32[16]{0:T(128)} %param.14) | copy-start | bytes 196
  95.9 14.1 %copy-start.3 = (f32[768]{0:T(1024)S(1)}, f32[768]{0:T(1024)}, u32[]{:S(2)}) copy-start(f32[768]{0:T(1024)} %param.18) | copy-start | bytes 9220
  95.9 14.1 %copy-start.4 = (f32[768]{0:T(1024)S(1)}, f32[768]{0:T(1024)}, u32[]{:S(2)}) copy-start(f32[768]{0:T(1024)} %param.19) | copy-start | bytes 9220
  100.9 27.1 %all-to-all-start.3 = ((bf16[32,24,384]{2,1,0:T(8,128)(2,1)}), bf16[32,24,384]{2,1,0:T(8,128)(2,1)S(1)}, u32[]{:S(2)}, u32[]{:S(2)}) async-start(bf16[32,24,384]{2,1,0:T(8,128)(2,1)} %upsample.1), calls=%async_computation.3 | async-start | bytes 1179648 | tf_op jit(solution)/shard_map/all_to_all | solution.py:313
  128.0 1.3 copy-start.2
Sparse Core Ops, SparseCore 0:
  10.0 89.0 all-gather.1
where the time goes:
time: 147 us
  waiting for transfers between devices  51.6 us (35%)
  starting transfers between devices  45.4 us (31%)
  Pallas kernels  20.2 us (14%)
  between operations  13.7 us (9%)
  local copies, waits for them, and re-layouts  10.6 us (7%)
  other arithmetic  5.23 us (4%)
    ppermute x8, waiting for transfers between devices, send(): return lax.ppermute(x, 'tm', turned(dz, dy, flip))  28.1 us
    all_to_all x1, waiting for transfers between devices, per_device(): arrived = lax.all_to_all(blocks, 'tm', 0, 0, tiled=True)  17.9 us
    ppermute x8, starting transfers between devices, send(): return lax.ppermute(x, 'tm', turned(dz, dy, flip))  17.6 us
    all_to_all x1, starting transfers between devices, per_device(): lax.all_to_all(jnp.broadcast_to(selected[None], (32,) + selected.shape),...  10.6 us
    pallas_call x1, Pallas kernels, per_device(): pl.pallas_call(residual_kernel, grid=(taps,), in_specs=[whole(32, 24, 8 *...  10.6 us
    all_to_all x1, starting transfers between devices, per_device(): arrived = lax.all_to_all(blocks, 'tm', 0, 0, tiled=True)  8.93 us
    unnamed x17, local copies, waits for them, and re-layouts  6.35 us
    pallas_call x1, Pallas kernels, per_device(): pl.pallas_call(upsample_kernel, grid_spec=pltpu.PrefetchScalarGridSpec(nu...  4.98 us
  transfers between devices with their start and end apart: 13, of which 6 were waited for; matrix products, arithmetic and copies ran while one was open for 8% of the time, Pallas kernels for 7%

commit v1 on v0

--- a/solution.py
+++ b/solution.py
@@ -73,23 +73,39 @@
     out_ref[0] = u.T[:width].astype(BF16)
 
 
-def history_kernel(h_ref, lat_ref, w_ref, a_ref, ia_ref, out_ref, wc_ref, v_ref):
+def cached_kernel(h_ref, w_ref, out_ref, wc_ref, v_ref):
+    fill_taps(w_ref, wc_ref)
+    rows = h_ref.shape[1]
+    past = 8
+    ht = h_ref[...].astype(F32).T.astype(BF16)
+    y = jnp.dot(ht, wc_ref[...], preferred_element_type=F32)
+    blank = jnp.zeros((past, y.shape[1]), F32)
+    for s in range(rows // past):
+        z = jnp.concatenate([y[past * s : past * (s + 1)], blank], axis=0)
+        v_ref[past * s : past * (s + 1), :] = tap_sum(z, 0, 48)[:past]
+    out_ref[...] = v_ref[...].astype(BF16)
+
+
+def history_kernel(
+    slot_ref, c_ref, lat_ref, w_ref, a_ref, ia_ref, out_ref, wc_ref, v_ref, all_ref
+):
     streams, frames, depth = lat_ref.shape
     width = out_ref.shape[1]
-    past = h_ref.shape[1] // streams
     half = streams // 2
+    past = 8
     fill_taps(w_ref, wc_ref)
-    wc = wc_ref[...]
-    ht = h_ref[...].astype(F32).T.astype(BF16)
-    yh = jnp.dot(ht, wc, preferred_element_type=F32)
-    yl = jnp.dot(
-        lat_ref[...].reshape(streams * frames, depth), wc, preferred_element_type=F32
+    y = jnp.dot(
+        lat_ref[...].reshape(streams * frames, depth),
+        wc_ref[...],
+        preferred_element_type=F32,
     )
+    all_ref[...] = c_ref[...].astype(F32)
+    blank = jnp.zeros((past, y.shape[1]), F32)
     for s in range(streams):
-        z = jnp.concatenate(
-            [yh[past * s : past * (s + 1)], yl[frames * s : frames * s + past]], axis=0
-        )
-        v_ref[past * s : past * (s + 1), :] = tap_sum(z, 0, width)[:past]
+        z = jnp.concatenate([blank, y[frames * s : frames * s + past]], axis=0)
+        at = pl.multiple_of(slot_ref[s] * past, past)
+        cached = all_ref[pl.ds(at, past), :]
+        v_ref[past * s : past * (s + 1), :] = tap_sum(z, 0, width)[:past] + cached
     for c in range(2):
         rows = [
             v_ref[pl.ds(c * half * past + i, half, stride=past), :] for i in range(past)
@@ -100,13 +116,14 @@
         out_ref[c] = u.T[:width].astype(BF16)
 
 
-def upsample_kernel(off_ref, x0, x1, x2, x3, xh_ref, w_ref, out_ref, xs_ref, fs_ref):
+def upsample_kernel(off_ref, *refs):
+    x_refs, (xh_ref, w_ref, out_ref, xs_ref, fs_ref) = refs[:8], refs[8:]
     width = 48
-    n = x0.shape[1]
-    pieces = x0.shape[0] // width
-    for dy, ref in enumerate((x0, x1, x2, x3)):
+    n = xs_ref.shape[1]
+    pieces = x_refs[0].shape[0] // width
+    for part, ref in enumerate(x_refs):
         for i in range(pieces):
-            at = pl.multiple_of(off_ref[dy * pieces + i], 16)
+            at = pl.multiple_of(off_ref[part * pieces + i], 16)
             xs_ref[pl.ds(at, width), :] = ref[i * width : (i + 1) * width, :]
     rows = w_ref.shape[0]
     half = rows // 2
@@ -180,6 +197,10 @@
                 ],
                 axis=1,
             ).astype(BF16)
+
+
+def after(x, *others):
+    return lax.optimization_barrier((x,) + others)[0]
 
 
 def whole(*shape):
@@ -227,15 +248,10 @@
         jnp.concatenate([up_other, up_t], axis=1),
     ).reshape(-1, up_t.shape[2])
 
-    flat = cache_prev.reshape(groups, past * slab)
-    every = lax.all_to_all(
-        jnp.broadcast_to(flat[None], (8,) + flat.shape), "stream", 0, 0, tiled=True
-    ).reshape(8 * groups, past * slab)
-    selected = jnp.take(every, prev_slot, axis=0).reshape(groups * past, slab).T
-    history = lax.all_to_all(
-        jnp.broadcast_to(selected[None], (32,) + selected.shape), "tm", 0, 0, tiled=True
+    flat = jnp.transpose(cache_prev, (2, 0, 1)).reshape(slab, groups * past)
+    cached = lax.all_to_all(
+        jnp.broadcast_to(flat[None], (32,) + flat.shape), "tm", 0, 0, tiled=True
     ).reshape(32 * slab, groups * past)
-
     pad = 128 - width
     alpha_c = jnp.pad(alpha_coarse, (0, pad), constant_values=1.0)[None]
     inverse_c = 1.0 / alpha_c
@@ -262,25 +278,50 @@
         name="coarse_main",
     )(order, latents, conv_in_w, alpha_c, inverse_c)
     own = jnp.concatenate([main[0], send(main[1], 0, 0, 1)], axis=0)
-    column = jnp.concatenate([own, send(own, 1, 0), send(own, 2, 0), send(own, 3, 0)], axis=0)
-    columns = [column, send(column, 0, 1), send(column, 0, 2), send(column, 0, 3)]
+    cached = after(cached, own)
+    added = pl.pallas_call(
+        cached_kernel,
+        grid=(1,),
+        in_specs=[whole(depth, groups * past), whole(taps, depth, width)],
+        out_specs=whole(groups * past, 128),
+        out_shape=jax.ShapeDtypeStruct((groups * past, 128), BF16),
+        scratch_shapes=[pltpu.VMEM((depth, 512), BF16), pltpu.VMEM((groups * past, 128), F32)],
+        compiler_params=pltpu.CompilerParams(vmem_limit_bytes=VMEM_LIMIT),
+        name="cached",
+    )(cached, conv_in_w)
+    every = lax.all_to_all(
+        jnp.broadcast_to(added[None], (8,) + added.shape), "stream", 0, 0, tiled=True
+    ).reshape(8 * groups * past, 128)
+    low = jnp.concatenate([own, send(own, 1, 0)], axis=0)
+    high = jnp.concatenate([send(own, 2, 0), send(own, 3, 0)], axis=0)
+    up_low, down_low = send(low, 0, 1), send(low, 0, 3)
+    up_high, down_high = send(high, 0, 1), send(high, 0, 3)
+    far_low, far_high = send(up_low, 0, 1), send(down_high, 0, 3)
+    columns = [low, high, up_low, up_high, far_low, far_high, down_low, down_high]
 
     head = pl.pallas_call(
         history_kernel,
-        grid=(1,),
-        in_specs=[
-            whole(depth, groups * past),
-            whole(groups, 16, depth),
-            whole(taps, depth, width),
-            whole(1, 128),
-            whole(1, 128),
-        ],
-        out_specs=whole(2, width, 128),
+        grid_spec=pltpu.PrefetchScalarGridSpec(
+            num_scalar_prefetch=1,
+            grid=(1,),
+            in_specs=[
+                whole(8 * groups * past, 128),
+                whole(groups, 16, depth),
+                whole(taps, depth, width),
+                whole(1, 128),
+                whole(1, 128),
+            ],
+            out_specs=whole(2, width, 128),
+            scratch_shapes=[
+                pltpu.VMEM((depth, 512), BF16),
+                pltpu.VMEM((groups * past, 128), F32),
+                pltpu.VMEM((8 * groups * past, 128), F32),
+            ],
+        ),
         out_shape=jax.ShapeDtypeStruct((2, width, 128), BF16),
-        scratch_shapes=[pltpu.VMEM((depth, 512), BF16), pltpu.VMEM((groups * past, 128), F32)],
         compiler_params=pltpu.CompilerParams(vmem_limit_bytes=VMEM_LIMIT),
         name="coarse_history",
-    )(history, latents, conv_in_w, alpha_c, inverse_c)
+    )(prev_slot, every, latents, conv_in_w, alpha_c, inverse_c)
     heads = lax.all_to_all(
         jnp.tile(head, (16, 1, 1)), "tm", 0, 0, tiled=True
     ).reshape(32 * width, 128)
@@ -298,7 +339,7 @@
         grid_spec=pltpu.PrefetchScalarGridSpec(
             num_scalar_prefetch=1,
             grid=(1,),
-            in_specs=[whole(8 * width, n)] * 4
+            in_specs=[whole(4 * width, n)] * 8
             + [whole(32 * width, 128), whole(16 * width, 32 * width)],
             out_specs=whole(32, 24, 8 * width),
             scratch_shapes=[
@@ -307,7 +348,7 @@
             ],
         ),
         out_shape=jax.ShapeDtypeStruct((32, 24, 8 * width), BF16),
-        compiler_params=pltpu.CompilerParams(vmem_limit_bytes=VMEM_LIMIT),
+        compiler_params=pltpu.CompilerParams(vmem_limit_bytes=60 * 1024 * 1024),
         name="upsample",
     )(offsets, *columns, heads, up)
     arrived = lax.all_to_all(blocks, "tm", 0, 0, tiled=True)

time: 147 us -> 143 us (0.973)
  waiting for transfers between devices: 51.6 us -> 45 us
  Pallas kernels: 20.2 us -> 23 us
    ppermute x8 -> x11, waiting for transfers between devices: 28.1 us -> 18.3 us  [send(): return lax.ppermute(x, 'tm', turned(dz, dy, flip))]
    ppermute x8 -> x11, starting transfers between devices: 17.6 us -> 11.4 us  [send(): return lax.ppermute(x, 'tm', turned(dz, dy, flip))]
    all_to_all x1, starting transfers between devices: 4.55 us -> 9.72 us  [per_device(): lax.all_to_all(jnp.tile(head, (16, 1, 1)), 'tm', 0, 0, tiled=True)]
    all_to_all x2, starting transfers between devices: 14.3 us -> 17 us  [the longest x1 12.8 us: per_device(): lax.all_to_all(jnp.broadcast_to(flat[None], (32,) + flat.shape), 'tm', 0,...]
    all_to_all x2, waiting for transfers between devices: 4.79 us -> 7.26 us  [the longest x1 4.22 us: per_device(): lax.all_to_all(jnp.broadcast_to(flat[None], (32,) + flat.shape), 'tm', 0,...]
    pallas_call x1, Pallas kernels: 4.98 us -> 6.55 us  [per_device(): pl.pallas_call(upsample_kernel, grid_spec=pltpu.PrefetchScalarGridSpec(nu...]
    unnamed x17 -> x40, local copies, waits for them, and re-layouts: 6.35 us -> 5.88 us
  transfers between devices with their start and end apart: 13 -> 16, of which waited for: 6 -> 9; matrix products, arithmetic and copies ran while one was open for 8% -> 8% of each run, Pallas kernels for 7% -> 9%
where the time goes in v1:
time: 143 us; the launch traced here: 142 us
  starting transfers between devices  45.6 us (32%)
  waiting for transfers between devices  45 us (31%)
  Pallas kernels  23 us (16%)
  between operations  13.9 us (10%)
  local copies, waits for them, and re-layouts  9.77 us (7%)
  other arithmetic  4.94 us (3%)
    all_to_all x1, waiting for transfers between devices, per_device(): arrived = lax.all_to_all(blocks, 'tm', 0, 0, tiled=True)  18.8 us
    ppermute x11, waiting for transfers between devices, send(): return lax.ppermute(x, 'tm', turned(dz, dy, flip))  18.3 us
    all_to_all x1, starting transfers between devices, per_device(): lax.all_to_all(jnp.broadcast_to(flat[None], (32,) + flat.shape), 'tm', 0,...  12.8 us
    ppermute x11, starting transfers between devices, send(): return lax.ppermute(x, 'tm', turned(dz, dy, flip))  11.4 us
    pallas_call x1, Pallas kernels, per_device(): pl.pallas_call(residual_kernel, grid=(taps,), in_specs=[whole(32, 24, 8 *...  10.6 us
    all_to_all x1, starting transfers between devices, per_device(): lax.all_to_all(jnp.tile(head, (16, 1, 1)), 'tm', 0, 0, tiled=True)  9.72 us
    all_to_all x1, starting transfers between devices, per_device(): arrived = lax.all_to_all(blocks, 'tm', 0, 0, tiled=True)  7.51 us
    pallas_call x1, Pallas kernels, per_device(): pl.pallas_call(upsample_kernel, grid_spec=pltpu.PrefetchScalarGridSpec(nu...  6.55 us
  transfers between devices with their start and end apart: 16, of which 9 were waited for; matrix products, arithmetic and copies ran while one was open for 8% of the time, Pallas kernels for 9%

profile of v1, /device:TPU:1, one launch (start us, length us, event | category | flops | bytes accessed | tf_op | source)
XLA Modules:
  0.0 142.3 jit_solution(4398162458471412766)
XLA Ops:
  6.5 0.0 all-gather.2.cloned.1.call-start
  6.5 0.7 all-gather.2.cloned.1.call-update
  7.3 0.8 copy.17
  8.1 0.8 broadcast_in_dim.30
  8.8 12.8 %all-to-all-start = ((bf16[32,32,128]{2,1,0:T(8,128)(2,1)}), bf16[32,32,128]{2,1,0:T(8,128)(2,1)S(1)}, u32[]{:S(2)}, u32[]{:S(2)}) async-start(bf16[32,32,128]{2,1,0:T(8,128)(2,1)} %broadcast_in_dim.30), calls=%async_computation | async-start | bytes 524288 | tf_op jit(solution)/shard_map/all_to_all | solution.py:252
  21.6 0.3 collective-permute-start.10
  21.9 0.1 pad_add_fusion.order_ref
  22.0 1.9 %copy.16.w_ref = bf16[7,1024,48]{2,1,0:T(8,128)(2,1)S(1)} copy(bf16[7,1024,48]{1,2,0:T(8,128)(2,1)} %param.15) | data formatting | bytes 1376256 | tf_op args[4]
  23.9 0.0 copy-done.17
  23.9 0.0 copy-start
  23.9 1.6 %copy-done = bf16[16,64,1024]{2,1,0:T(8,128)(2,1)S(1)} copy-done((bf16[16,64,1024]{2,1,0:T(8,128)(2,1)S(1)}, bf16[16,64,1024]{2,1,0:T(8,128)(2,1)}, u32[]{:S(2)}) %copy-start) | copy-done | bytes 2097176
  25.5 3.3 %coarse_main.1 = bf16[2,48,512]{2,1,0:T(8,128)(2,1)S(1)} custom-call(s32[2]{0:T(128)S(1)} %pad_add_fusion.order_ref, bf16[16,64,1024]{2,1,0:T(8,128)(2,1)S(1)} %copy-done, bf16[7,1024,48]{2,1,0:T(8,128)(2,1)S(1)} %copy.16.w_ref, f32[1,128]{1,0:T(1,128)S(1)} %get-tuple-element.10.a_ref, f32[1,128]{1,0:T(1,128)S(1)} %get-tuple-element.9.ia_ref), custom_call_target="tpu_custom_call" | custom-call | tf_op jit(solution)/shard_map/coarse_main/pallas_call | solution.py:259
  28.8 0.0 copy-start.3
  28.8 0.4 collective-permute-start
  29.2 1.0 collective-permute-done
  30.2 0.7 pad_maximum_fusion.1
  30.8 4.2 %all-to-all-done = bf16[32,32,128]{2,1,0:T(8,128)(2,1)S(1)} async-done(((bf16[32,32,128]{2,1,0:T(8,128)(2,1)}), bf16[32,32,128]{2,1,0:T(8,128)(2,1)S(1)}, u32[]{:S(2)}, u32[]{:S(2)}) %all-to-all-start) | async-done | bytes 262176 | tf_op jit(solution)/shard_map/all_to_all | solution.py:252
  35.1 1.0 cached.1
  36.0 0.7 broadcast_in_dim.31
  36.8 4.2 %all-to-all-start.1 = ((bf16[8,128,128]{2,1,0:T(8,128)(2,1)}), bf16[8,128,128]{2,1,0:T(8,128)(2,1)S(1)}, u32[]{:S(2)}, u32[]{:S(2)}) async-start(bf16[8,128,128]{2,1,0:T(8,128)(2,1)} %broadcast_in_dim.31), calls=%async_computation.1 | async-start | bytes 524288 | tf_op jit(solution)/shard_map/all_to_all | solution.py:292
  41.0 1.4 %collective-permute-start.2 = (bf16[96,512]{1,0:T(8,128)(2,1)}, bf16[96,512]{1,0:T(8,128)(2,1)S(1)}, u32[]{:S(2)}, u32[]{:S(2)}) collective-permute-start(bf16[96,512]{1,0:T(8,128)(2,1)} %pad_maximum_fusion.1), channel_id=1, source_target_pairs={{0,16},{1,17},{2,18},{3,19},{4,20},{5,21},{6,22},{7,23},{8,24},{9,... | collective-permute-start | bytes 294920 | tf_op jit(solution)/shard_map/ppermute | solution.py:240
  42.5 2.7 %collective-permute-start.3 = (bf16[96,512]{1,0:T(8,128)(2,1)}, bf16[96,512]{1,0:T(8,128)(2,1)S(1)}, u32[]{:S(2)}, u32[]{:S(2)}) collective-permute-start(bf16[96,512]{1,0:T(8,128)(2,1)} %pad_maximum_fusion.1), channel_id=1, source_target_pairs={{0,24},{1,25},{2,26},{3,27},{4,28},{5,29},{6,30},{7,31},{8,0},{9,1... | collective-permute-start | bytes 294920 | tf_op jit(solution)/shard_map/ppermute | solution.py:240
  45.2 0.0 collective-permute-start.1
  45.2 3.0 %all-to-all-done.1 = bf16[8,128,128]{2,1,0:T(8,128)(2,1)S(1)} async-done(((bf16[8,128,128]{2,1,0:T(8,128)(2,1)}), bf16[8,128,128]{2,1,0:T(8,128)(2,1)S(1)}, u32[]{:S(2)}, u32[]{:S(2)}) %all-to-all-start.1) | async-done | bytes 262176 | tf_op jit(solution)/shard_map/all_to_all | solution.py:292
  48.2 0.0 copy-done.14
  48.2 0.0 copy-done.3
  48.2 1.6 %copy-done.1 = bf16[16,64,1024]{2,1,0:T(8,128)(2,1)S(1)} copy-done((bf16[16,64,1024]{2,1,0:T(8,128)(2,1)S(1)}, bf16[16,64,1024]{2,1,0:T(8,128)(2,1)}, u32[]{:S(2)}) %copy-start.1) | copy-done | bytes 2097176
  49.8 1.6 %coarse_history.1 = bf16[2,48,128]{2,1,0:T(8,128)(2,1)S(1)} custom-call(s32[16]{0:T(128)S(1)} %copy-done.3, bf16[1024,128]{1,0:T(8,128)(2,1)S(1)} %bitcast.51, bf16[16,64,1024]{2,1,0:T(8,128)(2,1)S(1)} %copy-done.1, bf16[7,1024,48]{2,1,0:T(8,128)(2,1)S(1)} %copy.16.w_ref, f32[1,128]{1,0:T(1,128)S(1)} %get-tuple-element.10.a_ref, ...), custom_call_target="tpu_custom_call" | custom-call | tf_op jit(solution)/shard_map/coarse_history/pallas_call | solution.py:302
  51.4 0.8 tile.6
  52.2 9.7 %all-to-all-start.2 = ((bf16[32,48,128]{2,1,0:T(8,128)(2,1)}), bf16[32,48,128]{2,1,0:T(8,128)(2,1)S(1)}, u32[]{:S(2)}, u32[]{:S(2)}) async-start(bf16[32,48,128]{2,1,0:T(8,128)(2,1)} %bitcast.42), calls=%async_computation.2 | async-start | bytes 786432 | tf_op jit(solution)/shard_map/all_to_all | solution.py:325
  62.0 0.0 collective-permute-done.2
  62.0 0.0 collective-permute-done.3
  62.0 0.0 copy-start.7
  62.0 2.7 %collective-permute-start.7 = (bf16[192,512]{1,0:T(8,128)(2,1)S(1)}, bf16[192,512]{1,0:T(8,128)(2,1)S(1)}, u32[]{:S(2)}, u32[]{:S(2)}) collective-permute-start(bf16[192,512]{1,0:T(8,128)(2,1)S(1)} %constant_dynamic-update-slice_fusion.refs_1_), channel_id=1, source_target_pairs={{0,6},{1,7},{2,0},{3,1},{4,2},{5,3},{6,4},{7,5},{8,14},{9,15},{10,... | collective-permute-start | bytes 589832 | tf_op jit(solution)/shard_map/ppermute | solution.py:240
  64.7 0.0 collective-permute-done.1
  64.7 0.9 pad_maximum_fusion.refs_0_
  65.6 0.0 copy-start.6
  65.6 0.1 collective-permute-start.4
  66.0 0.6 stack.140.off_ref
  66.6 0.0 collective-permute-start.5
  66.6 2.7 %collective-permute-start.9 = (bf16[192,512]{1,0:T(8,128)(2,1)S(1)}, bf16[192,512]{1,0:T(8,128)(2,1)S(1)}, u32[]{:S(2)}, u32[]{:S(2)}) collective-permute-start(bf16[192,512]{1,0:T(8,128)(2,1)S(1)} %pad_maximum_fusion.refs_0_), channel_id=1, source_target_pairs={{0,6},{1,7},{2,0},{3,1},{4,2},{5,3},{6,4},{7,5},{8,14},{9,15},{10,... | collective-permute-start | bytes 589832 | tf_op jit(solution)/shard_map/ppermute | solution.py:240
  69.3 4.9 %collective-permute-done.7.refs_7_ = bf16[192,512]{1,0:T(8,128)(2,1)S(1)} collective-permute-done((bf16[192,512]{1,0:T(8,128)(2,1)S(1)}, bf16[192,512]{1,0:T(8,128)(2,1)S(1)}, u32[]{:S(2)}, u32[]{:S(2)}) %collective-permute-start.7) | collective-permute-done | bytes 196640 | tf_op jit(solution)/shard_map/ppermute | solution.py:240
  74.2 1.1 collective-permute-start.8
  75.3 1.5 %collective-permute-done.4.refs_2_ = bf16[192,512]{1,0:T(8,128)(2,1)S(1)} collective-permute-done((bf16[192,512]{1,0:T(8,128)(2,1)S(1)}, bf16[192,512]{1,0:T(8,128)(2,1)S(1)}, u32[]{:S(2)}, u32[]{:S(2)}) %collective-permute-start.4) | collective-permute-done | bytes 196640 | tf_op jit(solution)/shard_map/ppermute | solution.py:240
  76.7 0.0 collective-permute-start.6
  76.7 0.0 collective-permute-done.10
  76.8 3.3 %maximum_select_fusion = bf16[16,48,1536]{2,1,0:T(8,128)(2,1)} fusion(bf16[16,24,1536]{2,1,0:T(8,128)(2,1)} %collective-permute-done.10, bf16[16,24,1536]{2,1,0:T(8,128)(2,1)S(1)} %bitcast.56, pred[]{:T(512)S(6)} %eq.102), kind=kLoop, calls=%fused_computation | loop fusion | flops 10616832 | bytes 4718593 | tf_op jit(solution)/shard_map/jit(_where)/select_n | solution.py:245
  80.0 0.0 copy-done.7
  80.0 0.0 copy-done.8
  80.0 3.4 %collective-permute-done.5.refs_3_ = bf16[192,512]{1,0:T(8,128)(2,1)S(1)} collective-permute-done((bf16[192,512]{1,0:T(8,128)(2,1)S(1)}, bf16[192,512]{1,0:T(8,128)(2,1)S(1)}, u32[]{:S(2)}, u32[]{:S(2)}) %collective-permute-start.5) | collective-permute-done | bytes 196640 | tf_op jit(solution)/shard_map/ppermute | solution.py:240
  83.4 0.0 collective-permute-done.9.refs_6_
  83.4 3.8 %collective-permute-done.8.refs_5_ = bf16[192,512]{1,0:T(8,128)(2,1)S(1)} collective-permute-done((bf16[192,512]{1,0:T(8,128)(2,1)S(1)}, bf16[192,512]{1,0:T(8,128)(2,1)S(1)}, u32[]{:S(2)}, u32[]{:S(2)}) %collective-permute-start.8) | collective-permute-done | bytes 196640 | tf_op jit(solution)/shard_map/ppermute | solution.py:240
  87.2 3.8 %collective-permute-done.6.refs_4_ = bf16[192,512]{1,0:T(8,128)(2,1)S(1)} collective-permute-done((bf16[192,512]{1,0:T(8,128)(2,1)S(1)}, bf16[192,512]{1,0:T(8,128)(2,1)S(1)}, u32[]{:S(2)}, u32[]{:S(2)}) %collective-permute-start.6) | collective-permute-done | bytes 196640 | tf_op jit(solution)/shard_map/ppermute | solution.py:240
  91.0 0.0 all-to-all-done.2
  91.0 0.0 copy-done.11
  91.0 0.0 copy-done.12
  91.0 0.6 copy-done.13
  91.6 0.1 copy-done.4
  91.8 6.5 %upsample.1 = bf16[32,24,384]{2,1,0:T(8,128)(2,1)} custom-call(s32[32]{0:T(128)} %stack.140.off_ref, bf16[192,512]{1,0:T(8,128)(2,1)} %copy-done.6, bf16[192,512]{1,0:T(8,128)(2,1)} %copy-done.7, bf16[192,512]{1,0:T(8,128)(2,1)} %copy-done.9, bf16[192,512]{1,0:T(8,128)(2,1)} %copy-done.10, bf16[192,512]{1,0:T(8,128)(2,1)} %copy-done.13, ...), custom_call_target="tpu_custom_call" | custom-call | tf_op jit(solution)/shard_map/upsample/pallas_call | solution.py:337
  98.3 7.5 %all-to-all-start.3 = ((bf16[32,24,384]{2,1,0:T(8,128)(2,1)}), bf16[32,24,384]{2,1,0:T(8,128)(2,1)S(1)}, u32[]{:S(2)}, u32[]{:S(2)}) async-start(bf16[32,24,384]{2,1,0:T(8,128)(2,1)} %upsample.1), calls=%async_computation.3 | async-start | bytes 1179648 | tf_op jit(solution)/shard_map/all_to_all | solution.py:354
  105.9 0.1 broadcast_in_dim_tile.4.lim_ref
  106.0 0.0 copy-done.16
  106.1 18.8 %all-to-all-done.3.arr_ref = bf16[32,24,384]{2,1,0:T(8,128)(2,1)S(1)} async-done(((bf16[32,24,384]{2,1,0:T(8,128)(2,1)}), bf16[32,24,384]{2,1,0:T(8,128)(2,1)S(1)}, u32[]{:S(2)}, u32[]{:S(2)}) %all-to-all-start.3) | async-done | bytes 589856 | tf_op jit(solution)/shard_map/all_to_all | solution.py:354
  124.9 10.6 %residual.1 = bf16[16,16,768]{2,1,0:T(8,128)(2,1)} custom-call(bf16[32,24,384]{2,1,0:T(8,128)(2,1)S(1)} %all-to-all-done.3.arr_ref, s32[256,1]{1,0:T(8,128)S(1)} %broadcast_in_dim_tile.4.lim_ref, f32[1,768]{1,0:T(1,128)S(1)} %broadcast_in_dim.32.ai_ref, f32[1,768]{1,0:T(1,128)S(1)} %broadcast_in_dim.33.iai_ref, f32[1,768]{1,0:T(1,128)S(1)} %broadcast_in_dim.34.am_ref, ...), custom_call_target="tpu_custom_call" | custom-call | tf_op jit(solution)/shard_map/residual/pallas_call | solution.py:360
  (35 shorter events, 0.1 us)
Async XLA Ops:
  6.5 17.3 %copy-start.17 = (f32[48]{0:T(128)S(1)}, f32[48]{0:T(128)}, u32[]{:S(2)}) copy-start(f32[48]{0:T(128)} %param.17) | copy-start | bytes 580
  6.5 118.3 %all-gather.2.cloned.1.call-start = ((), (), s32[]{:S(2)}) async-start(), calls=%async_computation.4 | async-start | bytes 8515584 | tf_op jit(solution)/shard_map/all_gather | solution.py:242
  8.8 26.2 %all-to-all-start = ((bf16[32,32,128]{2,1,0:T(8,128)(2,1)}), bf16[32,32,128]{2,1,0:T(8,128)(2,1)S(1)}, u32[]{:S(2)}, u32[]{:S(2)}) async-start(bf16[32,32,128]{2,1,0:T(8,128)(2,1)} %broadcast_in_dim.30), calls=%async_computation | async-start | bytes 524288 | tf_op jit(solution)/shard_map/all_to_all | solution.py:252
  21.6 55.1 %collective-permute-start.10 = (bf16[16,24,1536]{2,1,0:T(8,128)(2,1)}, bf16[16,24,1536]{2,1,0:T(8,128)(2,1)}, u32[]{:S(2)}, u32[]{:S(2)}) collective-permute-start(bf16[16,24,1536]{2,1,0:T(8,128)(2,1)} %bitcast.55), channel_id=1, source_target_pairs={{0,1},{1,0},{2,3},{3,2},{4,5},{5,4},{6,7},{7,6},{8,9},{9,8},{10,11... | collective-permute-start | bytes 3538952 | tf_op jit(solution)/shard_map/ppermute | solution.py:240
  23.9 1.6 %copy-start = (bf16[16,64,1024]{2,1,0:T(8,128)(2,1)S(1)}, bf16[16,64,1024]{2,1,0:T(8,128)(2,1)}, u32[]{:S(2)}) copy-start(bf16[16,64,1024]{2,1,0:T(8,128)(2,1)} %lat_ref.3) | copy-start | bytes 6291460
  28.8 19.4 %copy-start.3 = (s32[16]{0:T(128)S(1)}, s32[16]{0:T(128)}, u32[]{:S(2)}) copy-start(s32[16]{0:T(128)} %slot_ref.1) | copy-start | bytes 196
  28.8 1.3 collective-permute-start
  30.2 18.1 %copy-start.14 = (bf16[48,512]{1,0:T(8,128)(2,1)}, bf16[48,512]{1,0:T(8,128)(2,1)S(1)}, u32[]{:S(2)}) copy-start(bf16[48,512]{1,0:T(8,128)(2,1)S(1)} %collective-permute-done) | copy-start | bytes 147460
  36.8 11.5 %all-to-all-start.1 = ((bf16[8,128,128]{2,1,0:T(8,128)(2,1)}), bf16[8,128,128]{2,1,0:T(8,128)(2,1)S(1)}, u32[]{:S(2)}, u32[]{:S(2)}) async-start(bf16[8,128,128]{2,1,0:T(8,128)(2,1)} %broadcast_in_dim.31), calls=%async_computation.1 | async-start | bytes 524288 | tf_op jit(solution)/shard_map/all_to_all | solution.py:292
  41.0 21.0 %collective-permute-start.2 = (bf16[96,512]{1,0:T(8,128)(2,1)}, bf16[96,512]{1,0:T(8,128)(2,1)S(1)}, u32[]{:S(2)}, u32[]{:S(2)}) collective-permute-start(bf16[96,512]{1,0:T(8,128)(2,1)} %pad_maximum_fusion.1), channel_id=1, source_target_pairs={{0,16},{1,17},{2,18},{3,19},{4,20},{5,21},{6,22},{7,23},{8,24},{9,... | collective-permute-start | bytes 294920 | tf_op jit(solution)/shard_map/ppermute | solution.py:240
  42.5 19.5 %collective-permute-start.3 = (bf16[96,512]{1,0:T(8,128)(2,1)}, bf16[96,512]{1,0:T(8,128)(2,1)S(1)}, u32[]{:S(2)}, u32[]{:S(2)}) collective-permute-start(bf16[96,512]{1,0:T(8,128)(2,1)} %pad_maximum_fusion.1), channel_id=1, source_target_pairs={{0,24},{1,25},{2,26},{3,27},{4,28},{5,29},{6,30},{7,31},{8,0},{9,1... | collective-permute-start | bytes 294920 | tf_op jit(solution)/shard_map/ppermute | solution.py:240
  45.2 19.5 %collective-permute-start.1 = (bf16[96,512]{1,0:T(8,128)(2,1)}, bf16[96,512]{1,0:T(8,128)(2,1)}, u32[]{:S(2)}, u32[]{:S(2)}) collective-permute-start(bf16[96,512]{1,0:T(8,128)(2,1)} %pad_maximum_fusion.1), channel_id=1, source_target_pairs={{0,8},{1,9},{2,10},{3,11},{4,12},{5,13},{6,14},{7,15},{8,16},{9,17... | collective-permute-start | bytes 294920 | tf_op jit(solution)/shard_map/ppermute | solution.py:240
  48.2 1.6 %copy-start.1 = (bf16[16,64,1024]{2,1,0:T(8,128)(2,1)S(1)}, bf16[16,64,1024]{2,1,0:T(8,128)(2,1)}, u32[]{:S(2)}) copy-start(bf16[16,64,1024]{2,1,0:T(8,128)(2,1)} %lat_ref.3) | copy-start | bytes 6291460
  49.8 26.9 %copy-start.5 = (bf16[16,1536,24]{1,2,0:T(8,128)(2,1)S(1)}, bf16[16,1536,24]{1,2,0:T(8,128)(2,1)}, u32[]{:S(2)}) copy-start(bf16[16,1536,24]{1,2,0:T(8,128)(2,1)} %param.16) | copy-start | bytes 3538948
  52.2 38.7 %all-to-all-start.2 = ((bf16[32,48,128]{2,1,0:T(8,128)(2,1)}), bf16[32,48,128]{2,1,0:T(8,128)(2,1)S(1)}, u32[]{:S(2)}, u32[]{:S(2)}) async-start(bf16[32,48,128]{2,1,0:T(8,128)(2,1)} %bitcast.42), calls=%async_computation.2 | async-start | bytes 786432 | tf_op jit(solution)/shard_map/all_to_all | solution.py:325
  62.0 18.0 %copy-start.7 = (bf16[192,512]{1,0:T(8,128)(2,1)}, bf16[192,512]{1,0:T(8,128)(2,1)S(1)}, u32[]{:S(2)}) copy-start(bf16[192,512]{1,0:T(8,128)(2,1)S(1)} %constant_dynamic-update-slice_fusion.refs_1_) | copy-start | bytes 589828
  62.0 12.1 %collective-permute-start.7 = (bf16[192,512]{1,0:T(8,128)(2,1)S(1)}, bf16[192,512]{1,0:T(8,128)(2,1)S(1)}, u32[]{:S(2)}, u32[]{:S(2)}) collective-permute-start(bf16[192,512]{1,0:T(8,128)(2,1)S(1)} %constant_dynamic-update-slice_fusion.refs_1_), channel_id=1, source_target_pairs={{0,6},{1,7},{2,0},{3,1},{4,2},{5,3},{6,4},{7,5},{8,14},{9,15},{10,... | collective-permute-start | bytes 589832 | tf_op jit(solution)/shard_map/ppermute | solution.py:240
  65.6 14.4 %copy-start.6 = (bf16[192,512]{1,0:T(8,128)(2,1)}, bf16[192,512]{1,0:T(8,128)(2,1)S(1)}, u32[]{:S(2)}) copy-start(bf16[192,512]{1,0:T(8,128)(2,1)S(1)} %pad_maximum_fusion.refs_0_) | copy-start | bytes 589828
  65.6 11.1 %collective-permute-start.4 = (bf16[192,512]{1,0:T(8,128)(2,1)S(1)}, bf16[192,512]{1,0:T(8,128)(2,1)S(1)}, u32[]{:S(2)}, u32[]{:S(2)}) collective-permute-start(bf16[192,512]{1,0:T(8,128)(2,1)S(1)} %pad_maximum_fusion.refs_0_), channel_id=1, source_target_pairs={{0,2},{1,3},{2,4},{3,5},{4,6},{5,7},{6,0},{7,1},{8,10},{9,11},{10,... | collective-permute-start | bytes 589832 | tf_op jit(solution)/shard_map/ppermute | solution.py:240
  66.6 16.8 %collective-permute-start.5 = (bf16[192,512]{1,0:T(8,128)(2,1)S(1)}, bf16[192,512]{1,0:T(8,128)(2,1)S(1)}, u32[]{:S(2)}, u32[]{:S(2)}) collective-permute-start(bf16[192,512]{1,0:T(8,128)(2,1)S(1)} %constant_dynamic-update-slice_fusion.refs_1_), channel_id=1, source_target_pairs={{0,2},{1,3},{2,4},{3,5},{4,6},{5,7},{6,0},{7,1},{8,10},{9,11},{10,... | collective-permute-start | bytes 589832 | tf_op jit(solution)/shard_map/ppermute | solution.py:240
  66.6 16.8 %collective-permute-start.9 = (bf16[192,512]{1,0:T(8,128)(2,1)S(1)}, bf16[192,512]{1,0:T(8,128)(2,1)S(1)}, u32[]{:S(2)}, u32[]{:S(2)}) collective-permute-start(bf16[192,512]{1,0:T(8,128)(2,1)S(1)} %pad_maximum_fusion.refs_0_), channel_id=1, source_target_pairs={{0,6},{1,7},{2,0},{3,1},{4,2},{5,3},{6,4},{7,5},{8,14},{9,15},{10,... | collective-permute-start | bytes 589832 | tf_op jit(solution)/shard_map/ppermute | solution.py:240
  74.2 5.9 %copy-start.8 = (bf16[192,512]{1,0:T(8,128)(2,1)}, bf16[192,512]{1,0:T(8,128)(2,1)S(1)}, u32[]{:S(2)}) copy-start(bf16[192,512]{1,0:T(8,128)(2,1)S(1)} %collective-permute-done.7.refs_7_) | copy-start | bytes 589828
  74.2 13.0 %collective-permute-start.8 = (bf16[192,512]{1,0:T(8,128)(2,1)S(1)}, bf16[192,512]{1,0:T(8,128)(2,1)S(1)}, u32[]{:S(2)}, u32[]{:S(2)}) collective-permute-start(bf16[192,512]{1,0:T(8,128)(2,1)S(1)} %collective-permute-done.7.refs_7_), channel_id=1, source_target_pairs={{0,6},{1,7},{2,0},{3,1},{4,2},{5,3},{6,4},{7,5},{8,14},{9,15},{10,... | collective-permute-start | bytes 589832 | tf_op jit(solution)/shard_map/ppermute | solution.py:240
  76.7 3.3 %copy-start.9 = (bf16[192,512]{1,0:T(8,128)(2,1)}, bf16[192,512]{1,0:T(8,128)(2,1)S(1)}, u32[]{:S(2)}) copy-start(bf16[192,512]{1,0:T(8,128)(2,1)S(1)} %collective-permute-done.4.refs_2_) | copy-start | bytes 589828
  76.7 14.2 %collective-permute-start.6 = (bf16[192,512]{1,0:T(8,128)(2,1)S(1)}, bf16[192,512]{1,0:T(8,128)(2,1)S(1)}, u32[]{:S(2)}, u32[]{:S(2)}) collective-permute-start(bf16[192,512]{1,0:T(8,128)(2,1)S(1)} %collective-permute-done.4.refs_2_), channel_id=1, source_target_pairs={{0,2},{1,3},{2,4},{3,5},{4,6},{5,7},{6,0},{7,1},{8,10},{9,11},{10,... | collective-permute-start | bytes 589832 | tf_op jit(solution)/shard_map/ppermute | solution.py:240
  83.4 7.6 %copy-start.10 = (bf16[192,512]{1,0:T(8,128)(2,1)}, bf16[192,512]{1,0:T(8,128)(2,1)S(1)}, u32[]{:S(2)}) copy-start(bf16[192,512]{1,0:T(8,128)(2,1)S(1)} %collective-permute-done.5.refs_3_) | copy-start | bytes 589828
  83.4 7.6 %copy-start.11 = (bf16[192,512]{1,0:T(8,128)(2,1)}, bf16[192,512]{1,0:T(8,128)(2,1)S(1)}, u32[]{:S(2)}) copy-start(bf16[192,512]{1,0:T(8,128)(2,1)S(1)} %collective-permute-done.9.refs_6_) | copy-start | bytes 589828
  87.2 3.8 %copy-start.12 = (bf16[192,512]{1,0:T(8,128)(2,1)}, bf16[192,512]{1,0:T(8,128)(2,1)S(1)}, u32[]{:S(2)}) copy-start(bf16[192,512]{1,0:T(8,128)(2,1)S(1)} %collective-permute-done.8.refs_5_) | copy-start | bytes 589828
  91.0 0.7 copy-start.13
  91.0 0.8 copy-start.4
  91.8 14.1 %copy-start.18 = (s32[16]{0:T(128)S(1)}, s32[16]{0:T(128)}, u32[]{:S(2)}) copy-start(s32[16]{0:T(128)} %param.14) | copy-start | bytes 196
  91.8 14.2 %copy-start.15 = (f32[768]{0:T(1024)S(1)}, f32[768]{0:T(1024)}, u32[]{:S(2)}) copy-start(f32[768]{0:T(1024)} %param.18) | copy-start | bytes 9220
  91.8 14.3 %copy-start.16 = (f32[768]{0:T(1024)S(1)}, f32[768]{0:T(1024)}, u32[]{:S(2)}) copy-start(f32[768]{0:T(1024)} %param.19) | copy-start | bytes 9220
  91.8 33.1 %copy-start.2 = (bf16[768,768]{1,0:T(8,128)(2,1)S(1)}, bf16[768,768]{1,0:T(8,128)(2,1)}, u32[]{:S(2)}) copy-start(bf16[768,768]{1,0:T(8,128)(2,1)} %wp_ref.1) | copy-start | bytes 3538948
  98.3 26.6 %all-to-all-start.3 = ((bf16[32,24,384]{2,1,0:T(8,128)(2,1)}), bf16[32,24,384]{2,1,0:T(8,128)(2,1)S(1)}, u32[]{:S(2)}, u32[]{:S(2)}) async-start(bf16[32,24,384]{2,1,0:T(8,128)(2,1)} %upsample.1), calls=%async_computation.3 | async-start | bytes 1179648 | tf_op jit(solution)/shard_map/all_to_all | solution.py:354
Sparse Core Ops, SparseCore 0:
  10.0 91.6 all-gather.1

commit v2 on v1

--- a/solution.py
+++ b/solution.py
@@ -146,57 +146,59 @@
 
 
 def residual_kernel(
-    arr_ref, lim_ref, ai_ref, iai_ref, am_ref, iam_ref, wd_ref, wp_ref,
-    out_ref, f_ref, win_ref, acc_ref, r_ref,
+    arr_ref, lim_ref, ai_ref, iai_ref, am_ref, iam_ref, wd_hbm, wp_ref,
+    out_ref, f_ref, win_ref, r_ref, wd_ref, sems,
 ):
-    k = pl.program_id(0)
-    taps = pl.num_programs(0)
-    rows, channels = acc_ref.shape
-    streams = out_ref.shape[0]
+    streams, shard, channels = out_ref.shape
+    rows = streams * shard
     sources, take, _ = arr_ref.shape
+    taps = wd_ref.shape[0]
     piece = 48
     half = streams // 2
-
-    @pl.when(k == 0)
-    def _():
-        for c in range(2):
-            for j in range(8):
-                x = jnp.concatenate(
-                    [
-                        arr_ref[m, :, piece * j : piece * (j + 1)].astype(F32)
-                        for m in range(c, sources, 2)
-                    ],
-                    axis=1,
-                )
-                for t in range(take // half):
-                    at = (8 * t + j) * streams + half * c
-                    f_ref[at : at + half, :] = x[half * t : half * (t + 1)]
-        win_ref[...] = snake(f_ref[...], ai_ref[...], iai_ref[...]).astype(BF16)
-        acc_ref[...] = jnp.zeros_like(acc_ref)
-
-    at = pl.multiple_of((k + 2) * streams, 16)
-    acc_ref[...] += jnp.dot(
-        win_ref[pl.ds(at, rows), :], wd_ref[0], preferred_element_type=F32
-    )
-
-    @pl.when(k == taps - 1)
-    def _():
-        middle = snake(acc_ref[...], am_ref[...], iam_ref[...]).astype(BF16)
-        summed = f_ref[8 * streams :, :] + jnp.dot(
-            middle, wp_ref[...], preferred_element_type=F32
-        )
-        local = lax.broadcasted_iota(jnp.int32, (rows, channels), 0) // streams
-        kept = jnp.where(local < lim_ref[...], summed, 0.0)
-        for g in range(channels // 128):
-            r_ref[g] = kept[:, 128 * g : 128 * (g + 1)]
-        for s in range(streams):
-            out_ref[s] = jnp.concatenate(
+    copies = [
+        pltpu.make_async_copy(wd_hbm.at[k], wd_ref.at[k], sems.at[k])
+        for k in range(taps)
+    ]
+    for copy in copies:
+        copy.start()
+    for c in range(2):
+        for j in range(8):
+            x = jnp.concatenate(
                 [
-                    r_ref[g, pl.ds(s, rows // streams, stride=streams), :]
-                    for g in range(channels // 128)
+                    arr_ref[m, :, piece * j : piece * (j + 1)].astype(F32)
+                    for m in range(c, sources, 2)
                 ],
                 axis=1,
-            ).astype(BF16)
+            )
+            for t in range(take // half):
+                at = (8 * t + j) * streams + half * c
+                f_ref[at : at + half, :] = x[half * t : half * (t + 1)]
+    used = 2 * streams
+    win_ref[used:, :] = snake(f_ref[used:, :], ai_ref[...], iai_ref[...]).astype(BF16)
+    total = None
+    for k in range(taps):
+        copies[k].wait()
+        at = (k + 2) * streams
+        part = jnp.dot(
+            win_ref[at : at + rows, :], wd_ref[k], preferred_element_type=F32
+        )
+        total = part if total is None else total + part
+    middle = snake(total, am_ref[...], iam_ref[...]).astype(BF16)
+    summed = f_ref[8 * streams :, :] + jnp.dot(
+        middle, wp_ref[...], preferred_element_type=F32
+    )
+    local = lax.broadcasted_iota(jnp.int32, (rows, channels), 0) // streams
+    kept = jnp.where(local < lim_ref[...], summed, 0.0)
+    for g in range(channels // 128):
+        r_ref[g] = kept[:, 128 * g : 128 * (g + 1)]
+    for s in range(streams):
+        out_ref[s] = jnp.concatenate(
+            [
+                r_ref[g, pl.ds(s, shard, stride=streams), :]
+                for g in range(channels // 128)
+            ],
+            axis=1,
+        ).astype(BF16)
 
 
 def after(x, *others):
@@ -359,7 +361,7 @@
     limit = jnp.tile(limit, shard)[:, None].astype(jnp.int32)
     return pl.pallas_call(
         residual_kernel,
-        grid=(taps,),
+        grid=(1,),
         in_specs=[
             whole(32, 24, 8 * width),
             whole(rows, 1),
@@ -367,7 +369,7 @@
             whole(1, channels),
             whole(1, channels),
             whole(1, channels),
-            pl.BlockSpec((1, channels, channels), lambda k: (k, 0, 0)),
+            pl.BlockSpec(memory_space=pl.ANY),
             whole(channels, channels),
         ],
         out_specs=whole(groups, shard, channels),
@@ -375,8 +377,9 @@
         scratch_shapes=[
             pltpu.VMEM((24 * groups, channels), F32),
             pltpu.VMEM((24 * groups, channels), BF16),
-            pltpu.VMEM((rows, channels), F32),
             pltpu.VMEM((channels // 128, rows, 128), F32),
+            pltpu.VMEM((taps, channels, channels), BF16),
+            pltpu.SemaphoreType.DMA((taps,)),
         ],
         compiler_params=pltpu.CompilerParams(vmem_limit_bytes=VMEM_LIMIT),
         name="residual",

time: 143 us -> 140 us (0.979)
  Pallas kernels: 23 us -> 20.3 us
    pallas_call x1, Pallas kernels: 10.6 us -> 7.84 us  [per_device(): pl.pallas_call(residual_kernel, grid=(1,), in_specs=[whole(32, 24, 8 * wi...]
where the time goes in v2:
time: 140 us
  starting transfers between devices  45.6 us (33%)
  waiting for transfers between devices  45 us (32%)
  Pallas kernels  20.3 us (14%)
  between operations  14 us (10%)
  local copies, waits for them, and re-layouts  9.77 us (7%)
  other arithmetic  4.94 us (4%)
    all_to_all x1, waiting for transfers between devices, per_device(): arrived = lax.all_to_all(blocks, 'tm', 0, 0, tiled=True)  18.8 us
    ppermute x11, waiting for transfers between devices, send(): return lax.ppermute(x, 'tm', turned(dz, dy, flip))  18.3 us
    all_to_all x1, starting transfers between devices, per_device(): lax.all_to_all(jnp.broadcast_to(flat[None], (32,) + flat.shape), 'tm', 0,...  12.8 us
    ppermute x11, starting transfers between devices, send(): return lax.ppermute(x, 'tm', turned(dz, dy, flip))  11.4 us
    all_to_all x1, starting transfers between devices, per_device(): lax.all_to_all(jnp.tile(head, (16, 1, 1)), 'tm', 0, 0, tiled=True)  9.72 us
    pallas_call x1, Pallas kernels, per_device(): pl.pallas_call(residual_kernel, grid=(1,), in_specs=[whole(32, 24, 8 * wi...  7.84 us
    all_to_all x1, starting transfers between devices, per_device(): arrived = lax.all_to_all(blocks, 'tm', 0, 0, tiled=True)  7.51 us
    pallas_call x1, Pallas kernels, per_device(): pl.pallas_call(upsample_kernel, grid_spec=pltpu.PrefetchScalarGridSpec(nu...  6.55 us
  transfers between devices with their start and end apart: 16, of which 9 were waited for; matrix products, arithmetic and copies ran while one was open for 8% of the time, Pallas kernels for 9%

profile of v2, /device:TPU:1, one launch (start us, length us, event | category | flops | bytes accessed | tf_op | source)
XLA Modules:
  0.0 139.6 jit_solution(2929022124120041563)
XLA Ops:
  6.5 0.0 all-gather.2.cloned.1.call-start
  6.5 0.7 all-gather.2.cloned.1.call-update
  7.3 0.8 copy.17
  8.1 0.8 broadcast_in_dim.30
  8.8 12.8 %all-to-all-start = ((bf16[32,32,128]{2,1,0:T(8,128)(2,1)}), bf16[32,32,128]{2,1,0:T(8,128)(2,1)S(1)}, u32[]{:S(2)}, u32[]{:S(2)}) async-start(bf16[32,32,128]{2,1,0:T(8,128)(2,1)} %broadcast_in_dim.30), calls=%async_computation | async-start | bytes 524288 | tf_op jit(solution)/shard_map/all_to_all | solution.py:254
  21.6 0.3 collective-permute-start.10
  21.9 0.1 pad_add_fusion.order_ref
  22.0 1.9 %copy.16.w_ref = bf16[7,1024,48]{2,1,0:T(8,128)(2,1)S(1)} copy(bf16[7,1024,48]{1,2,0:T(8,128)(2,1)} %param.15) | data formatting | bytes 1376256 | tf_op args[4]
  23.9 0.0 copy-done.17
  23.9 0.0 copy-start
  23.9 1.6 %copy-done = bf16[16,64,1024]{2,1,0:T(8,128)(2,1)S(1)} copy-done((bf16[16,64,1024]{2,1,0:T(8,128)(2,1)S(1)}, bf16[16,64,1024]{2,1,0:T(8,128)(2,1)}, u32[]{:S(2)}) %copy-start) | copy-done | bytes 2097176
  25.5 3.3 %coarse_main.1 = bf16[2,48,512]{2,1,0:T(8,128)(2,1)S(1)} custom-call(s32[2]{0:T(128)S(1)} %pad_add_fusion.order_ref, bf16[16,64,1024]{2,1,0:T(8,128)(2,1)S(1)} %copy-done, bf16[7,1024,48]{2,1,0:T(8,128)(2,1)S(1)} %copy.16.w_ref, f32[1,128]{1,0:T(1,128)S(1)} %get-tuple-element.10.a_ref, f32[1,128]{1,0:T(1,128)S(1)} %get-tuple-element.9.ia_ref), custom_call_target="tpu_custom_call" | custom-call | tf_op jit(solution)/shard_map/coarse_main/pallas_call | solution.py:261
  28.8 0.0 copy-start.3
  28.8 0.4 collective-permute-start
  29.2 1.0 collective-permute-done
  30.2 0.7 pad_maximum_fusion.1
  30.8 4.2 %all-to-all-done = bf16[32,32,128]{2,1,0:T(8,128)(2,1)S(1)} async-done(((bf16[32,32,128]{2,1,0:T(8,128)(2,1)}), bf16[32,32,128]{2,1,0:T(8,128)(2,1)S(1)}, u32[]{:S(2)}, u32[]{:S(2)}) %all-to-all-start) | async-done | bytes 262176 | tf_op jit(solution)/shard_map/all_to_all | solution.py:254
  35.1 1.0 cached.1
  36.0 0.7 broadcast_in_dim.31
  36.8 4.2 %all-to-all-start.1 = ((bf16[8,128,128]{2,1,0:T(8,128)(2,1)}), bf16[8,128,128]{2,1,0:T(8,128)(2,1)S(1)}, u32[]{:S(2)}, u32[]{:S(2)}) async-start(bf16[8,128,128]{2,1,0:T(8,128)(2,1)} %broadcast_in_dim.31), calls=%async_computation.1 | async-start | bytes 524288 | tf_op jit(solution)/shard_map/all_to_all | solution.py:294
  41.0 1.4 %collective-permute-start.2 = (bf16[96,512]{1,0:T(8,128)(2,1)}, bf16[96,512]{1,0:T(8,128)(2,1)S(1)}, u32[]{:S(2)}, u32[]{:S(2)}) collective-permute-start(bf16[96,512]{1,0:T(8,128)(2,1)} %pad_maximum_fusion.1), channel_id=1, source_target_pairs={{0,16},{1,17},{2,18},{3,19},{4,20},{5,21},{6,22},{7,23},{8,24},{9,... | collective-permute-start | bytes 294920 | tf_op jit(solution)/shard_map/ppermute | solution.py:242
  42.5 2.7 %collective-permute-start.3 = (bf16[96,512]{1,0:T(8,128)(2,1)}, bf16[96,512]{1,0:T(8,128)(2,1)S(1)}, u32[]{:S(2)}, u32[]{:S(2)}) collective-permute-start(bf16[96,512]{1,0:T(8,128)(2,1)} %pad_maximum_fusion.1), channel_id=1, source_target_pairs={{0,24},{1,25},{2,26},{3,27},{4,28},{5,29},{6,30},{7,31},{8,0},{9,1... | collective-permute-start | bytes 294920 | tf_op jit(solution)/shard_map/ppermute | solution.py:242
  45.2 0.0 collective-permute-start.1
  45.2 3.0 %all-to-all-done.1 = bf16[8,128,128]{2,1,0:T(8,128)(2,1)S(1)} async-done(((bf16[8,128,128]{2,1,0:T(8,128)(2,1)}), bf16[8,128,128]{2,1,0:T(8,128)(2,1)S(1)}, u32[]{:S(2)}, u32[]{:S(2)}) %all-to-all-start.1) | async-done | bytes 262176 | tf_op jit(solution)/shard_map/all_to_all | solution.py:294
  48.2 0.0 copy-done.14
  48.2 0.0 copy-done.3
  48.2 1.6 %copy-done.1 = bf16[16,64,1024]{2,1,0:T(8,128)(2,1)S(1)} copy-done((bf16[16,64,1024]{2,1,0:T(8,128)(2,1)S(1)}, bf16[16,64,1024]{2,1,0:T(8,128)(2,1)}, u32[]{:S(2)}) %copy-start.1) | copy-done | bytes 2097176
  49.8 1.6 %coarse_history.1 = bf16[2,48,128]{2,1,0:T(8,128)(2,1)S(1)} custom-call(s32[16]{0:T(128)S(1)} %copy-done.3, bf16[1024,128]{1,0:T(8,128)(2,1)S(1)} %bitcast.51, bf16[16,64,1024]{2,1,0:T(8,128)(2,1)S(1)} %copy-done.1, bf16[7,1024,48]{2,1,0:T(8,128)(2,1)S(1)} %copy.16.w_ref, f32[1,128]{1,0:T(1,128)S(1)} %get-tuple-element.10.a_ref, ...), custom_call_target="tpu_custom_call" | custom-call | tf_op jit(solution)/shard_map/coarse_history/pallas_call | solution.py:304
  51.4 0.8 tile.6
  52.2 9.7 %all-to-all-start.2 = ((bf16[32,48,128]{2,1,0:T(8,128)(2,1)}), bf16[32,48,128]{2,1,0:T(8,128)(2,1)S(1)}, u32[]{:S(2)}, u32[]{:S(2)}) async-start(bf16[32,48,128]{2,1,0:T(8,128)(2,1)} %bitcast.42), calls=%async_computation.2 | async-start | bytes 786432 | tf_op jit(solution)/shard_map/all_to_all | solution.py:327
  62.0 0.0 collective-permute-done.2
  62.0 0.0 collective-permute-done.3
  62.0 0.0 copy-start.7
  62.0 2.7 %collective-permute-start.7 = (bf16[192,512]{1,0:T(8,128)(2,1)S(1)}, bf16[192,512]{1,0:T(8,128)(2,1)S(1)}, u32[]{:S(2)}, u32[]{:S(2)}) collective-permute-start(bf16[192,512]{1,0:T(8,128)(2,1)S(1)} %constant_dynamic-update-slice_fusion.refs_1_), channel_id=1, source_target_pairs={{0,6},{1,7},{2,0},{3,1},{4,2},{5,3},{6,4},{7,5},{8,14},{9,15},{10,... | collective-permute-start | bytes 589832 | tf_op jit(solution)/shard_map/ppermute | solution.py:242
  64.7 0.0 collective-permute-done.1
  64.7 0.9 pad_maximum_fusion.refs_0_
  65.6 0.0 copy-start.6
  65.6 0.1 collective-permute-start.4
  66.0 0.6 stack.140.off_ref
  66.6 0.0 collective-permute-start.5
  66.6 2.7 %collective-permute-start.9 = (bf16[192,512]{1,0:T(8,128)(2,1)S(1)}, bf16[192,512]{1,0:T(8,128)(2,1)S(1)}, u32[]{:S(2)}, u32[]{:S(2)}) collective-permute-start(bf16[192,512]{1,0:T(8,128)(2,1)S(1)} %pad_maximum_fusion.refs_0_), channel_id=1, source_target_pairs={{0,6},{1,7},{2,0},{3,1},{4,2},{5,3},{6,4},{7,5},{8,14},{9,15},{10,... | collective-permute-start | bytes 589832 | tf_op jit(solution)/shard_map/ppermute | solution.py:242
  69.3 4.9 %collective-permute-done.7.refs_7_ = bf16[192,512]{1,0:T(8,128)(2,1)S(1)} collective-permute-done((bf16[192,512]{1,0:T(8,128)(2,1)S(1)}, bf16[192,512]{1,0:T(8,128)(2,1)S(1)}, u32[]{:S(2)}, u32[]{:S(2)}) %collective-permute-start.7) | collective-permute-done | bytes 196640 | tf_op jit(solution)/shard_map/ppermute | solution.py:242
  74.2 1.1 collective-permute-start.8
  75.3 1.5 %collective-permute-done.4.refs_2_ = bf16[192,512]{1,0:T(8,128)(2,1)S(1)} collective-permute-done((bf16[192,512]{1,0:T(8,128)(2,1)S(1)}, bf16[192,512]{1,0:T(8,128)(2,1)S(1)}, u32[]{:S(2)}, u32[]{:S(2)}) %collective-permute-start.4) | collective-permute-done | bytes 196640 | tf_op jit(solution)/shard_map/ppermute | solution.py:242
  76.7 0.0 collective-permute-start.6
  76.7 0.0 collective-permute-done.10
  76.7 0.0 copy-done.5
  76.8 3.3 %maximum_select_fusion = bf16[16,48,1536]{2,1,0:T(8,128)(2,1)} fusion(bf16[16,24,1536]{2,1,0:T(8,128)(2,1)} %collective-permute-done.10, bf16[16,24,1536]{2,1,0:T(8,128)(2,1)S(1)} %bitcast.56, pred[]{:T(512)S(6)} %eq.102), kind=kLoop, calls=%fused_computation | loop fusion | flops 10616832 | bytes 4718593 | tf_op jit(solution)/shard_map/jit(_where)/select_n | solution.py:247
  80.0 0.0 copy-done.9
  80.0 3.4 %collective-permute-done.5.refs_3_ = bf16[192,512]{1,0:T(8,128)(2,1)S(1)} collective-permute-done((bf16[192,512]{1,0:T(8,128)(2,1)S(1)}, bf16[192,512]{1,0:T(8,128)(2,1)S(1)}, u32[]{:S(2)}, u32[]{:S(2)}) %collective-permute-start.5) | collective-permute-done | bytes 196640 | tf_op jit(solution)/shard_map/ppermute | solution.py:242
  83.4 0.0 collective-permute-done.9.refs_6_
  83.4 3.8 %collective-permute-done.8.refs_5_ = bf16[192,512]{1,0:T(8,128)(2,1)S(1)} collective-permute-done((bf16[192,512]{1,0:T(8,128)(2,1)S(1)}, bf16[192,512]{1,0:T(8,128)(2,1)S(1)}, u32[]{:S(2)}, u32[]{:S(2)}) %collective-permute-start.8) | collective-permute-done | bytes 196640 | tf_op jit(solution)/shard_map/ppermute | solution.py:242
  87.2 3.8 %collective-permute-done.6.refs_4_ = bf16[192,512]{1,0:T(8,128)(2,1)S(1)} collective-permute-done((bf16[192,512]{1,0:T(8,128)(2,1)S(1)}, bf16[192,512]{1,0:T(8,128)(2,1)S(1)}, u32[]{:S(2)}, u32[]{:S(2)}) %collective-permute-start.6) | collective-permute-done | bytes 196640 | tf_op jit(solution)/shard_map/ppermute | solution.py:242
  91.0 0.0 all-to-all-done.2
  91.0 0.0 copy-done.10
  91.0 0.6 copy-done.13
  91.6 0.1 copy-done.4
  91.8 6.5 %upsample.1 = bf16[32,24,384]{2,1,0:T(8,128)(2,1)} custom-call(s32[32]{0:T(128)} %stack.140.off_ref, bf16[192,512]{1,0:T(8,128)(2,1)} %copy-done.6, bf16[192,512]{1,0:T(8,128)(2,1)} %copy-done.7, bf16[192,512]{1,0:T(8,128)(2,1)} %copy-done.9, bf16[192,512]{1,0:T(8,128)(2,1)} %copy-done.10, bf16[192,512]{1,0:T(8,128)(2,1)} %copy-done.13, ...), custom_call_target="tpu_custom_call" | custom-call | tf_op jit(solution)/shard_map/upsample/pallas_call | solution.py:339
  98.3 7.5 %all-to-all-start.3 = ((bf16[32,24,384]{2,1,0:T(8,128)(2,1)}), bf16[32,24,384]{2,1,0:T(8,128)(2,1)S(1)}, u32[]{:S(2)}, u32[]{:S(2)}) async-start(bf16[32,24,384]{2,1,0:T(8,128)(2,1)} %upsample.1), calls=%async_computation.3 | async-start | bytes 1179648 | tf_op jit(solution)/shard_map/all_to_all | solution.py:356
  105.8 0.0 copy-done.18
  105.9 0.1 broadcast_in_dim_tile.4.lim_ref
  106.1 18.8 %all-to-all-done.3.arr_ref = bf16[32,24,384]{2,1,0:T(8,128)(2,1)S(1)} async-done(((bf16[32,24,384]{2,1,0:T(8,128)(2,1)}), bf16[32,24,384]{2,1,0:T(8,128)(2,1)S(1)}, u32[]{:S(2)}, u32[]{:S(2)}) %all-to-all-start.3) | async-done | bytes 589856 | tf_op jit(solution)/shard_map/all_to_all | solution.py:356
  124.9 0.0 copy-done.2
  124.9 7.8 %residual.1 = bf16[16,16,768]{2,1,0:T(8,128)(2,1)} custom-call(bf16[32,24,384]{2,1,0:T(8,128)(2,1)S(1)} %all-to-all-done.3.arr_ref, s32[256,1]{1,0:T(8,128)S(1)} %broadcast_in_dim_tile.4.lim_ref, f32[1,768]{1,0:T(1,128)S(1)} %broadcast_in_dim.32.ai_ref, f32[1,768]{1,0:T(1,128)S(1)} %broadcast_in_dim.33.iai_ref, f32[1,768]{1,0:T(1,128)S(1)} %broadcast_in_dim.34.am_ref, ...), custom_call_target="tpu_custom_call" | custom-call | tf_op jit(solution)/shard_map/residual/pallas_call | solution.py:362
  (35 shorter events, 0.1 us)
Async XLA Ops:
  6.5 17.3 %copy-start.17 = (f32[48]{0:T(128)S(1)}, f32[48]{0:T(128)}, u32[]{:S(2)}) copy-start(f32[48]{0:T(128)} %param.17) | copy-start | bytes 580
  6.5 118.3 %all-gather.2.cloned.1.call-start = ((), (), s32[]{:S(2)}) async-start(), calls=%async_computation.4 | async-start | bytes 8515584 | tf_op jit(solution)/shard_map/all_gather | solution.py:244
  8.8 26.2 %all-to-all-start = ((bf16[32,32,128]{2,1,0:T(8,128)(2,1)}), bf16[32,32,128]{2,1,0:T(8,128)(2,1)S(1)}, u32[]{:S(2)}, u32[]{:S(2)}) async-start(bf16[32,32,128]{2,1,0:T(8,128)(2,1)} %broadcast_in_dim.30), calls=%async_computation | async-start | bytes 524288 | tf_op jit(solution)/shard_map/all_to_all | solution.py:254
  21.6 55.1 %collective-permute-start.10 = (bf16[16,24,1536]{2,1,0:T(8,128)(2,1)}, bf16[16,24,1536]{2,1,0:T(8,128)(2,1)}, u32[]{:S(2)}, u32[]{:S(2)}) collective-permute-start(bf16[16,24,1536]{2,1,0:T(8,128)(2,1)} %bitcast.55), channel_id=1, source_target_pairs={{0,1},{1,0},{2,3},{3,2},{4,5},{5,4},{6,7},{7,6},{8,9},{9,8},{10,11... | collective-permute-start | bytes 3538952 | tf_op jit(solution)/shard_map/ppermute | solution.py:242
  23.9 1.6 %copy-start = (bf16[16,64,1024]{2,1,0:T(8,128)(2,1)S(1)}, bf16[16,64,1024]{2,1,0:T(8,128)(2,1)}, u32[]{:S(2)}) copy-start(bf16[16,64,1024]{2,1,0:T(8,128)(2,1)} %lat_ref.3) | copy-start | bytes 6291460
  28.8 19.4 %copy-start.3 = (s32[16]{0:T(128)S(1)}, s32[16]{0:T(128)}, u32[]{:S(2)}) copy-start(s32[16]{0:T(128)} %slot_ref.1) | copy-start | bytes 196
  28.8 1.3 collective-permute-start
  30.2 18.1 %copy-start.14 = (bf16[48,512]{1,0:T(8,128)(2,1)}, bf16[48,512]{1,0:T(8,128)(2,1)S(1)}, u32[]{:S(2)}) copy-start(bf16[48,512]{1,0:T(8,128)(2,1)S(1)} %collective-permute-done) | copy-start | bytes 147460
  36.8 11.5 %all-to-all-start.1 = ((bf16[8,128,128]{2,1,0:T(8,128)(2,1)}), bf16[8,128,128]{2,1,0:T(8,128)(2,1)S(1)}, u32[]{:S(2)}, u32[]{:S(2)}) async-start(bf16[8,128,128]{2,1,0:T(8,128)(2,1)} %broadcast_in_dim.31), calls=%async_computation.1 | async-start | bytes 524288 | tf_op jit(solution)/shard_map/all_to_all | solution.py:294
  41.0 21.0 %collective-permute-start.2 = (bf16[96,512]{1,0:T(8,128)(2,1)}, bf16[96,512]{1,0:T(8,128)(2,1)S(1)}, u32[]{:S(2)}, u32[]{:S(2)}) collective-permute-start(bf16[96,512]{1,0:T(8,128)(2,1)} %pad_maximum_fusion.1), channel_id=1, source_target_pairs={{0,16},{1,17},{2,18},{3,19},{4,20},{5,21},{6,22},{7,23},{8,24},{9,... | collective-permute-start | bytes 294920 | tf_op jit(solution)/shard_map/ppermute | solution.py:242
  42.5 19.5 %collective-permute-start.3 = (bf16[96,512]{1,0:T(8,128)(2,1)}, bf16[96,512]{1,0:T(8,128)(2,1)S(1)}, u32[]{:S(2)}, u32[]{:S(2)}) collective-permute-start(bf16[96,512]{1,0:T(8,128)(2,1)} %pad_maximum_fusion.1), channel_id=1, source_target_pairs={{0,24},{1,25},{2,26},{3,27},{4,28},{5,29},{6,30},{7,31},{8,0},{9,1... | collective-permute-start | bytes 294920 | tf_op jit(solution)/shard_map/ppermute | solution.py:242
  45.2 19.5 %collective-permute-start.1 = (bf16[96,512]{1,0:T(8,128)(2,1)}, bf16[96,512]{1,0:T(8,128)(2,1)}, u32[]{:S(2)}, u32[]{:S(2)}) collective-permute-start(bf16[96,512]{1,0:T(8,128)(2,1)} %pad_maximum_fusion.1), channel_id=1, source_target_pairs={{0,8},{1,9},{2,10},{3,11},{4,12},{5,13},{6,14},{7,15},{8,16},{9,17... | collective-permute-start | bytes 294920 | tf_op jit(solution)/shard_map/ppermute | solution.py:242
  48.2 1.6 %copy-start.1 = (bf16[16,64,1024]{2,1,0:T(8,128)(2,1)S(1)}, bf16[16,64,1024]{2,1,0:T(8,128)(2,1)}, u32[]{:S(2)}) copy-start(bf16[16,64,1024]{2,1,0:T(8,128)(2,1)} %lat_ref.3) | copy-start | bytes 6291460
  49.8 26.9 %copy-start.5 = (bf16[16,1536,24]{1,2,0:T(8,128)(2,1)S(1)}, bf16[16,1536,24]{1,2,0:T(8,128)(2,1)}, u32[]{:S(2)}) copy-start(bf16[16,1536,24]{1,2,0:T(8,128)(2,1)} %param.16) | copy-start | bytes 3538948
  52.2 38.7 %all-to-all-start.2 = ((bf16[32,48,128]{2,1,0:T(8,128)(2,1)}), bf16[32,48,128]{2,1,0:T(8,128)(2,1)S(1)}, u32[]{:S(2)}, u32[]{:S(2)}) async-start(bf16[32,48,128]{2,1,0:T(8,128)(2,1)} %bitcast.42), calls=%async_computation.2 | async-start | bytes 786432 | tf_op jit(solution)/shard_map/all_to_all | solution.py:327
  62.0 18.0 %copy-start.7 = (bf16[192,512]{1,0:T(8,128)(2,1)}, bf16[192,512]{1,0:T(8,128)(2,1)S(1)}, u32[]{:S(2)}) copy-start(bf16[192,512]{1,0:T(8,128)(2,1)S(1)} %constant_dynamic-update-slice_fusion.refs_1_) | copy-start | bytes 589828
  62.0 12.1 %collective-permute-start.7 = (bf16[192,512]{1,0:T(8,128)(2,1)S(1)}, bf16[192,512]{1,0:T(8,128)(2,1)S(1)}, u32[]{:S(2)}, u32[]{:S(2)}) collective-permute-start(bf16[192,512]{1,0:T(8,128)(2,1)S(1)} %constant_dynamic-update-slice_fusion.refs_1_), channel_id=1, source_target_pairs={{0,6},{1,7},{2,0},{3,1},{4,2},{5,3},{6,4},{7,5},{8,14},{9,15},{10,... | collective-permute-start | bytes 589832 | tf_op jit(solution)/shard_map/ppermute | solution.py:242
  65.6 14.4 %copy-start.6 = (bf16[192,512]{1,0:T(8,128)(2,1)}, bf16[192,512]{1,0:T(8,128)(2,1)S(1)}, u32[]{:S(2)}) copy-start(bf16[192,512]{1,0:T(8,128)(2,1)S(1)} %pad_maximum_fusion.refs_0_) | copy-start | bytes 589828
  65.6 11.1 %collective-permute-start.4 = (bf16[192,512]{1,0:T(8,128)(2,1)S(1)}, bf16[192,512]{1,0:T(8,128)(2,1)S(1)}, u32[]{:S(2)}, u32[]{:S(2)}) collective-permute-start(bf16[192,512]{1,0:T(8,128)(2,1)S(1)} %pad_maximum_fusion.refs_0_), channel_id=1, source_target_pairs={{0,2},{1,3},{2,4},{3,5},{4,6},{5,7},{6,0},{7,1},{8,10},{9,11},{10,... | collective-permute-start | bytes 589832 | tf_op jit(solution)/shard_map/ppermute | solution.py:242
  66.6 16.8 %collective-permute-start.5 = (bf16[192,512]{1,0:T(8,128)(2,1)S(1)}, bf16[192,512]{1,0:T(8,128)(2,1)S(1)}, u32[]{:S(2)}, u32[]{:S(2)}) collective-permute-start(bf16[192,512]{1,0:T(8,128)(2,1)S(1)} %constant_dynamic-update-slice_fusion.refs_1_), channel_id=1, source_target_pairs={{0,2},{1,3},{2,4},{3,5},{4,6},{5,7},{6,0},{7,1},{8,10},{9,11},{10,... | collective-permute-start | bytes 589832 | tf_op jit(solution)/shard_map/ppermute | solution.py:242
  66.6 16.8 %collective-permute-start.9 = (bf16[192,512]{1,0:T(8,128)(2,1)S(1)}, bf16[192,512]{1,0:T(8,128)(2,1)S(1)}, u32[]{:S(2)}, u32[]{:S(2)}) collective-permute-start(bf16[192,512]{1,0:T(8,128)(2,1)S(1)} %pad_maximum_fusion.refs_0_), channel_id=1, source_target_pairs={{0,6},{1,7},{2,0},{3,1},{4,2},{5,3},{6,4},{7,5},{8,14},{9,15},{10,... | collective-permute-start | bytes 589832 | tf_op jit(solution)/shard_map/ppermute | solution.py:242
  74.2 5.9 %copy-start.8 = (bf16[192,512]{1,0:T(8,128)(2,1)}, bf16[192,512]{1,0:T(8,128)(2,1)S(1)}, u32[]{:S(2)}) copy-start(bf16[192,512]{1,0:T(8,128)(2,1)S(1)} %collective-permute-done.7.refs_7_) | copy-start | bytes 589828
  74.2 13.0 %collective-permute-start.8 = (bf16[192,512]{1,0:T(8,128)(2,1)S(1)}, bf16[192,512]{1,0:T(8,128)(2,1)S(1)}, u32[]{:S(2)}, u32[]{:S(2)}) collective-permute-start(bf16[192,512]{1,0:T(8,128)(2,1)S(1)} %collective-permute-done.7.refs_7_), channel_id=1, source_target_pairs={{0,6},{1,7},{2,0},{3,1},{4,2},{5,3},{6,4},{7,5},{8,14},{9,15},{10,... | collective-permute-start | bytes 589832 | tf_op jit(solution)/shard_map/ppermute | solution.py:242
  76.7 3.3 %copy-start.9 = (bf16[192,512]{1,0:T(8,128)(2,1)}, bf16[192,512]{1,0:T(8,128)(2,1)S(1)}, u32[]{:S(2)}) copy-start(bf16[192,512]{1,0:T(8,128)(2,1)S(1)} %collective-permute-done.4.refs_2_) | copy-start | bytes 589828
  76.7 14.2 %collective-permute-start.6 = (bf16[192,512]{1,0:T(8,128)(2,1)S(1)}, bf16[192,512]{1,0:T(8,128)(2,1)S(1)}, u32[]{:S(2)}, u32[]{:S(2)}) collective-permute-start(bf16[192,512]{1,0:T(8,128)(2,1)S(1)} %collective-permute-done.4.refs_2_), channel_id=1, source_target_pairs={{0,2},{1,3},{2,4},{3,5},{4,6},{5,7},{6,0},{7,1},{8,10},{9,11},{10,... | collective-permute-start | bytes 589832 | tf_op jit(solution)/shard_map/ppermute | solution.py:242
  83.4 7.6 %copy-start.10 = (bf16[192,512]{1,0:T(8,128)(2,1)}, bf16[192,512]{1,0:T(8,128)(2,1)S(1)}, u32[]{:S(2)}) copy-start(bf16[192,512]{1,0:T(8,128)(2,1)S(1)} %collective-permute-done.5.refs_3_) | copy-start | bytes 589828
  83.4 7.6 %copy-start.11 = (bf16[192,512]{1,0:T(8,128)(2,1)}, bf16[192,512]{1,0:T(8,128)(2,1)S(1)}, u32[]{:S(2)}) copy-start(bf16[192,512]{1,0:T(8,128)(2,1)S(1)} %collective-permute-done.9.refs_6_) | copy-start | bytes 589828
  87.2 3.8 %copy-start.12 = (bf16[192,512]{1,0:T(8,128)(2,1)}, bf16[192,512]{1,0:T(8,128)(2,1)S(1)}, u32[]{:S(2)}) copy-start(bf16[192,512]{1,0:T(8,128)(2,1)S(1)} %collective-permute-done.8.refs_5_) | copy-start | bytes 589828
  91.0 0.7 copy-start.13
  91.0 0.8 copy-start.4
  91.8 14.1 %copy-start.18 = (s32[16]{0:T(128)S(1)}, s32[16]{0:T(128)}, u32[]{:S(2)}) copy-start(s32[16]{0:T(128)} %param.14) | copy-start | bytes 196
  91.8 14.2 %copy-start.15 = (f32[768]{0:T(1024)S(1)}, f32[768]{0:T(1024)}, u32[]{:S(2)}) copy-start(f32[768]{0:T(1024)} %param.18) | copy-start | bytes 9220
  91.8 14.3 %copy-start.16 = (f32[768]{0:T(1024)S(1)}, f32[768]{0:T(1024)}, u32[]{:S(2)}) copy-start(f32[768]{0:T(1024)} %param.19) | copy-start | bytes 9220
  91.8 33.1 %copy-start.2 = (bf16[768,768]{1,0:T(8,128)(2,1)S(1)}, bf16[768,768]{1,0:T(8,128)(2,1)}, u32[]{:S(2)}) copy-start(bf16[768,768]{1,0:T(8,128)(2,1)} %wp_ref.1) | copy-start | bytes 3538948
  98.3 26.6 %all-to-all-start.3 = ((bf16[32,24,384]{2,1,0:T(8,128)(2,1)}), bf16[32,24,384]{2,1,0:T(8,128)(2,1)S(1)}, u32[]{:S(2)}, u32[]{:S(2)}) async-start(bf16[32,24,384]{2,1,0:T(8,128)(2,1)} %upsample.1), calls=%async_computation.3 | async-start | bytes 1179648 | tf_op jit(solution)/shard_map/all_to_all | solution.py:356
Sparse Core Ops, SparseCore 0:
  10.0 91.6 all-gather.1
